TPU v7x, 256 devices: a whole 4x4x8 slice. The times are simulated.
256 devices in a mesh: dp: 32 (over z, x_lo, core), fsdp: 8 (over x_hi, y).
Axes of the slice: x: 4 (x_hi: 2, x_lo: 2; x = x_hi * 2 + x_lo), y: 4, z: 8, core: 2. Of those that a mesh axis runs over, the one named last changes fastest.
Arguments:
- grads: bfloat16 [32, 2, 8192, 1024], P('dp', None, 'fsdp'), may hold values from -1.1953125 to 1.1953125
- raw_proj: float32 [2, 1024, 512], P(None, 'fsdp'), may hold values from -6 to 6
- bucket_owner: int32 [2, 512], P(None, 'fsdp'), may hold values from 0 to 31, as said below
- first_moment: float32 [2, 8, 128, 16, 512], P(None, 'fsdp', 'dp'), may hold values from -0.6 to 0.6
- second_moment: float32 [2, 8, 128, 16, 512], P(None, 'fsdp', 'dp'), may hold values from 0.01 to 0.05
Outputs:
- weight_delta: bfloat16 [2, 8192, 1024], P(None, 'fsdp')
- first_out: float32 [2, 8, 128, 16, 512], P(None, 'fsdp', 'dp')
- second_out: float32 [2, 8, 128, 16, 512], P(None, 'fsdp', 'dp')
Inputs may be any that keep to these rules, and one draw needn't show every extreme that they name: `bucket_owner`: within each matrix and each block of 64 buckets of one fsdp index, no owner holds more than 4 buckets, and one owner holds exactly 4.
All inputs are finite; a program needn't handle non-finite values.
Results may differ from a plain program's by a relative error of at most 0.0062.
Values may be sent and summed in bfloat16 or wider, within the bound.
A program may use at most 64 MiB of HBM per device.

v0:
```python
import jax
import jax.numpy as jnp
from jax import lax
from jax.sharding import PartitionSpec as P


def rows_at(table, index):
    return jax.vmap(lambda part_table, part_index: jnp.take(part_table, part_index, axis=0))(
        table, index
    )


def adam_update(first, second, grad_rows):
    new_first = 0.9 * first + 0.1 * grad_rows
    new_second = 0.999 * second + 0.001 * grad_rows * grad_rows
    scaled = (
        6.0 * (new_first / (1.0 - 0.9**10)) / (jnp.sqrt(new_second / (1.0 - 0.999**10)) + 1e-08)
    )
    return (new_first, new_second, scaled.astype(jnp.bfloat16))


def shards(grads, raw_proj, bucket_owner, first_moment, second_moment):
    matrices = grads.shape[1]
    local_rows = grads.shape[2]
    features = grads.shape[3]
    rank_width = raw_proj.shape[2]
    buckets = bucket_owner.shape[1]
    capacity = first_moment.shape[2]
    bucket_rows = local_rows // buckets
    replicas = lax.axis_size("dp")
    slot_total = replicas * capacity
    gram_part = jnp.einsum("mkr,mks->mrs", raw_proj, raw_proj, precision=lax.Precision.HIGHEST)
    gram = lax.psum(gram_part, "fsdp")
    factor = jnp.linalg.cholesky(gram)
    basis_part = lax.linalg.triangular_solve(
        factor, raw_proj, left_side=False, lower=True, transpose_a=True
    )
    basis = lax.all_gather(basis_part.astype(jnp.bfloat16), "fsdp", axis=1, tiled=True)
    projected = jnp.einsum("mdk,mkr->mdr", grads[0], basis, preferred_element_type=jnp.float32)
    blocks = projected.reshape(matrices, buckets, bucket_rows, rank_width)
    same = bucket_owner[:, :, None] == bucket_owner[:, None, :]
    earlier = jnp.arange(buckets)[None, :] < jnp.arange(buckets)[:, None]
    ranks = jnp.sum(jnp.logical_and(same, earlier).astype(jnp.int32), axis=-1)
    slots = bucket_owner * capacity + ranks
    slot_ids = jnp.arange(slot_total, dtype=jnp.int32)
    matches = slots[:, None, :] == slot_ids[None, :, None]
    occupied = jnp.any(matches, axis=2)
    bucket_of = jnp.sum(
        matches.astype(jnp.int32) * jnp.arange(buckets, dtype=jnp.int32)[None, None, :], axis=2
    )
    start = lax.axis_index("dp") * capacity
    occupied_mine = lax.dynamic_slice_in_dim(occupied, start, capacity, 1)
    totals = lax.psum(blocks, "dp")
    bucket_mine = lax.dynamic_slice_in_dim(bucket_of, start, capacity, 1)
    grad_rows = rows_at(totals, bucket_mine)
    first = first_moment[:, 0]
    second = second_moment[:, 0]
    new_first, new_second, update = adam_update(first, second, grad_rows)
    keep_mask = occupied_mine[:, :, None, None]
    first_out = jnp.where(keep_mask, new_first, first)[:, None]
    second_out = jnp.where(keep_mask, new_second, second)[:, None]
    owner_rows = jnp.einsum(
        "mcbr,mkr->mcbk", update, basis, preferred_element_type=jnp.float32
    ).astype(jnp.bfloat16)
    every_rows = lax.all_gather(owner_rows, "dp", axis=1, tiled=True)
    delta = rows_at(every_rows, slots)
    weight_delta = delta.reshape(matrices, local_rows, features)
    return (weight_delta, first_out, second_out)


def solution(mesh):
    return jax.shard_map(
        shards,
        mesh=mesh,
        in_specs=(
            P("dp", None, "fsdp", None),
            P(None, "fsdp", None),
            P(None, "fsdp"),
            P(None, "fsdp", "dp", None, None),
            P(None, "fsdp", "dp", None, None),
        ),
        out_specs=(
            P(None, "fsdp", None),
            P(None, "fsdp", "dp", None, None),
            P(None, "fsdp", "dp", None, None),
        ),
        check_vma=False,
    )
```

profile of v0, /device:TPU:1, one launch (start us, length us, event | category | flops | bytes accessed | tf_op | source)
XLA Modules:
  0.0 785.3 jit_solution(841170741054117501)
XLA Ops:
  7.2 4.3 fusion.70
  11.8 96.7 %all-reduce.4.cloned.1.call-done = f32[2,512,512]{1,2,0:T(8,128)} async-done(((f32[2,512,512]{1,2,0:T(8,128)}), f32[2,512,512]{1,2,0:T(8,128)}) %all-reduce.4.cloned.1.call-update) | async-done | bytes 2097168 | tf_op jit(solution)/shard_map/psum | solution.py:33
  108.4 3.0 copy.48
  111.5 2.1 fusion.7
  113.6 1.3 copy-done.1
  114.9 23.5 %custom-call.34 = f32[2,128,128]{2,1,0:T(8,128)S(1)} custom-call(f32[2,128,128]{2,1,0:T(8,128)S(1)} %cholesky.274), custom_call_target="Cholesky" | custom-call | tf_op jit(solution)/shard_map/jit(cholesky)/cholesky | solution.py:34
  138.4 19.7 %custom-call.35 = f32[2,1,128,128]{2,3,1,0:T(8,128)S(1)} custom-call(f32[2,1,128,128]{3,2,1,0:T(8,128)S(1)} %select_bitcast_fusion.2), custom_call_target="InvertDiagBlocksLowerTriangular" | custom-call | tf_op jit(solution)/shard_map/jit(cholesky)/cholesky | solution.py:34
  158.3 1.5 constant_dynamic-update-slice_fusion.3
  159.8 1.5 convolution_subtract_fusion
  161.4 23.5 %custom-call.36 = f32[2,128,128]{2,1,0:T(8,128)S(1)} custom-call(f32[2,128,128]{2,1,0:T(8,128)S(1)} %cholesky.278), custom_call_target="Cholesky" | custom-call | tf_op jit(solution)/shard_map/jit(cholesky)/cholesky | solution.py:34
  184.9 19.8 %custom-call.37 = f32[2,1,128,128]{2,3,1,0:T(8,128)S(1)} custom-call(f32[2,1,128,128]{3,2,1,0:T(8,128)S(1)} %get-tuple-element.32), custom_call_target="InvertDiagBlocksLowerTriangular" | custom-call | tf_op jit(solution)/shard_map/jit(cholesky)/cholesky | solution.py:34
  204.7 0.4 convolution_dynamic-update-slice_fusion
  205.1 1.6 convolution_subtract_fusion.1
  206.7 23.5 %custom-call.38 = f32[2,128,128]{2,1,0:T(8,128)S(1)} custom-call(f32[2,128,128]{2,1,0:T(8,128)S(1)} %cholesky.283), custom_call_target="Cholesky" | custom-call | tf_op jit(solution)/shard_map/jit(cholesky)/cholesky | solution.py:34
  230.2 19.7 %custom-call.39 = f32[2,1,128,128]{2,3,1,0:T(8,128)S(1)} custom-call(f32[2,1,128,128]{3,2,1,0:T(8,128)S(1)} %get-tuple-element.30), custom_call_target="InvertDiagBlocksLowerTriangular" | custom-call | tf_op jit(solution)/shard_map/jit(cholesky)/cholesky | solution.py:34
  249.8 0.3 convolution_dynamic-update-slice_fusion.1
  250.1 1.5 convolution_subtract_fusion.4
  251.7 23.7 %custom-call.40 = f32[2,128,128]{2,1,0:T(8,128)S(1)} custom-call(f32[2,128,128]{2,1,0:T(8,128)S(1)} %convolution_subtract_fusion.4), custom_call_target="Cholesky" | custom-call | tf_op jit(solution)/shard_map/jit(cholesky)/cholesky | solution.py:34
  275.7 1.7 select_select_fusion
  277.4 14.9 %while.1 = (s32[]{:T(128)}, f32[2,512,512]{2,1,0:T(8,128)}, s32[4,2]{0,1:T(2,128)S(1)}, f32[4,2,128,128]{3,2,0,1:T(8,128)}, s32[]{:T(128)}) while((s32[]{:T(128)}, f32[2,512,512]{2,1,0:T(8,128)}, s32[4,2]{0,1:T(2,128)S(1)}, f32[4,2,128,128]{3,2,0,1:T(8,128)}, s32[]{:T(128)}) %tuple.37), condition=%wide.while_cond, body=%wide.while_body.sunk | while | flops 2 | bytes 263777 | solution.py:35
  277.5 0.6 fusion.80
  278.1 3.1 bitcast_dynamic-update-slice_fusion.2
  281.3 0.6 fusion.80
  281.9 3.1 bitcast_dynamic-update-slice_fusion.2
  285.0 0.6 fusion.80
  285.6 3.1 bitcast_dynamic-update-slice_fusion.2
  288.7 0.6 fusion.80
  289.3 3.0 bitcast_dynamic-update-slice_fusion.2
  292.3 79.4 %custom-call.41 = f32[2,4,128,128]{2,3,1,0:T(8,128)S(1)} custom-call(f32[2,4,128,128]{3,2,1,0:T(8,128)} %bitcast.129), custom_call_target="InvertDiagBlocksLowerTriangular" | custom-call | tf_op jit(solution)/shard_map/triangular_solve | solution.py:35
  371.8 0.4 bitcast_convert_fusion
  372.2 1.3 convolution_subtract_fusion.5
  373.5 0.4 fusion.69
  373.9 1.6 convolution_subtract_fusion.3
  375.5 0.4 fusion.68
  375.9 1.8 convolution_subtract_fusion.2
  377.7 0.4 convolution_convert_fusion
  378.1 0.7 pad_maximum_fusion
  378.9 62.6 %all-gather.3.cloned.1.call-done = bf16[2,1024,512]{1,2,0:T(8,128)(2,1)} async-done(((bf16[2,128,512]{1,2,0:T(8,128)(2,1)}), bf16[2,1024,512]{1,2,0:T(8,128)(2,1)}) %all-gather.3.cloned.1.call-update) | async-done | bytes 2097168 | tf_op jit(solution)/shard_map/all_gather | solution.py:38
  441.5 7.2 fusion.2
  448.7 5.4 copy.63
  454.3 0.6 copy-done.6
  455.4 235.6 %all-reduce.6.cloned.1.call-done = f32[2,64,16,512]{3,2,1,0:T(8,128)} async-done(((f32[2,64,16,512]{3,2,1,0:T(8,128)}), f32[2,64,16,512]{3,2,1,0:T(8,128)}) %all-reduce.6.cloned.1.call-update) | async-done | bytes 4194320 | tf_op jit(solution)/shard_map/psum | solution.py:53
  691.0 2.8 gather_fusion
  693.8 1.4 fusion.8
  695.7 1.0 fusion.27
  696.7 71.6 %all-gather.5.cloned.1.call-done = bf16[2,128,16,1024]{3,2,1,0:T(8,128)(2,1)} async-done(((bf16[2,4,16,1024]{3,2,1,0:T(8,128)(2,1)}), bf16[2,128,16,1024]{3,2,1,0:T(8,128)(2,1)}) %all-gather.5.cloned.1.call-update) | async-done | bytes 8388624 | tf_op jit(solution)/shard_map/all_gather | solution.py:65
  768.3 6.3 gather_fusion.1
  774.5 3.9 bitcast_select_fusion
  (54 shorter events, 2.4 us)
Async XLA Ops:
  7.2 101.3 %all-reduce.4.cloned.1.call-start = ((), (), s32[]{:S(2)}) async-start(), calls=%async_computation | async-start | bytes 4194304 | tf_op jit(solution)/shard_map/psum | solution.py:33
  11.6 429.9 %all-gather.3.cloned.1.call-start = ((), (), s32[]{:S(2)}) async-start(), calls=%async_computation.1 | async-start | bytes 2359296 | tf_op jit(solution)/shard_map/all_gather | solution.py:38
  108.4 3.0 copy-start
  113.6 1.3 copy-start.1
  275.7 96.1 %copy-start.2 = (f32[2,128,512]{2,1,0:T(8,128)S(1)}, f32[2,128,512]{2,1,0:T(8,128)}, u32[]{:S(2)}) copy-start(f32[2,128,512]{2,1,0:T(8,128)} %param.6) | copy-start | bytes 1572868
  378.9 312.2 %all-reduce.6.cloned.1.call-start = ((), (), s32[]{:S(2)}) async-start(), calls=%async_computation.2 | async-start | bytes 8388608 | tf_op jit(solution)/shard_map/psum | solution.py:53
  454.1 0.7 copy-start.6
  454.1 239.6 %copy-start.3 = (bf16[2,1024,512]{1,2,0:T(8,128)(2,1)S(1)}, bf16[2,1024,512]{1,2,0:T(8,128)(2,1)}, u32[]{:S(2)}) copy-start(bf16[2,1024,512]{1,2,0:T(8,128)(2,1)} %all-gather.3.cloned.1.call-done) | copy-start | bytes 6291460
  454.2 239.6 %copy-start.4 = (f32[2,1,4,16,512]{4,3,2,1,0:T(8,128)S(1)}, f32[2,1,4,16,512]{4,3,2,1,0:T(8,128)}, u32[]{:S(2)}) copy-start(f32[2,1,4,16,512]{4,3,2,1,0:T(8,128)} %param.9) | copy-start | bytes 786436
  454.2 239.6 %copy-start.5 = (f32[2,1,4,16,512]{4,3,2,1,0:T(8,128)S(1)}, f32[2,1,4,16,512]{4,3,2,1,0:T(8,128)}, u32[]{:S(2)}) copy-start(f32[2,1,4,16,512]{4,3,2,1,0:T(8,128)} %param.8) | copy-start | bytes 786436
  454.2 314.1 %all-gather.5.cloned.1.call-start = ((), (), s32[]{:S(2)}) async-start(), calls=%async_computation.3 | async-start | bytes 8650752 | tf_op jit(solution)/shard_map/all_gather | solution.py:65
Sparse Core Ops, SparseCore 0:
  11.7 96.6 all-reduce.3
  379.0 62.5 all-gather.2
  454.3 236.6 all-reduce.5
  695.3 72.9 all-gather.4
where the time goes:
time: 796 us; the launch traced here: 785 us
  waiting for transfers between devices  467 us (59%)
  other arithmetic  243 us (31%)
  local copies, waits for them, and re-layouts  35 us (4%)
  matrix products  26 us (3%)
  between operations  14.5 us (2%)
    psum x1, waiting for transfers between devices, shards(): totals = lax.psum(blocks, 'dp')  236 us
    another operation x16, other arithmetic, shards(): factor = jnp.linalg.cholesky(gram)  154 us
    psum x1, waiting for transfers between devices, shards(): gram = lax.psum(gram_part, 'fsdp')  96.7 us
    another operation x5, other arithmetic, shards(): lax.linalg.triangular_solve(factor, raw_proj, left_side=False, lower=True...  82 us
    all_gather x1, waiting for transfers between devices, shards(): every_rows = lax.all_gather(owner_rows, 'dp', axis=1, tiled=True)  71.6 us
    all_gather x1, waiting for transfers between devices, shards(): lax.all_gather(basis_part.astype(jnp.bfloat16), 'fsdp', axis=1, tiled=True)  62.6 us
  transfers between devices with their start and end apart: 4, of which 4 were waited for; matrix products, arithmetic and copies ran while one was open for 0% of the time, Pallas kernels for 0%

commit v1 on v0

v1 whole, which is shorter than its diff:
```python
import jax
import jax.numpy as jnp
from jax import lax
from jax.experimental import pallas as pl
from jax.experimental.pallas import tpu as pltpu
from jax.sharding import PartitionSpec as P

HI = lax.Precision.HIGHEST
F32 = jnp.float32
BF16 = jnp.bfloat16
BLK = 128
NZ, NY, CAP, ROWS = 8, 4, 4, 16


def mm(a, b, ca, cb, precision=HI):
    return lax.dot_general(
        a, b, (((ca,), (cb,)), ((), ())), precision=precision, preferred_element_type=F32
    )


def panel(S, g):
    rows = pl.ds(pl.multiple_of(8 * g, 8), 8)
    V, W = S[rows, 0:BLK], S[rows, BLK : 2 * BLK]
    turned = pltpu.roll(V, lax.rem(BLK - 8 * g, BLK), 1)
    C = [jnp.broadcast_to(turned[:, k : k + 1], (8, BLK)) for k in range(8)]
    sub = lax.broadcasted_iota(jnp.int32, (8, BLK), 0)
    lane = lax.broadcasted_iota(jnp.int32, (8, BLK), 1)
    pivot = jnp.ones((8, BLK), F32)
    for j in range(8):
        p = jnp.broadcast_to(C[j][j : j + 1, :], (8, BLK))
        pivot = jnp.where(sub == j, p, pivot)
        if j < 7:
            m = jnp.where(sub > j, C[j] * (1.0 / p), 0.0)
            for k in range(j + 1, 8):
                C[k] = C[k] - m * jnp.broadcast_to(C[k][j : j + 1, :], (8, BLK))
            V = V - m * jnp.broadcast_to(V[j : j + 1, :], (8, BLK))
            W = W - m * jnp.broadcast_to(W[j : j + 1, :], (8, BLK))
    s = lax.rsqrt(pivot)
    s = s * (1.5 - 0.5 * pivot * s * s)
    VW = jnp.concatenate([V * s, W * s], axis=1)
    S[rows, :] = VW
    later = jnp.where(lane >= 8 * g + 8, VW[:, 0:BLK], 0.0)
    S[...] = S[...] - mm(later, VW, 0, 0)


def factor(A, X, S, Q, hooks):
    eye = (
        lax.broadcasted_iota(jnp.int32, (BLK, BLK), 0)
        == lax.broadcasted_iota(jnp.int32, (BLK, BLK), 1)
    ).astype(F32)
    blocks = A.shape[0] // BLK
    for k in range(blocks):
        lo, hi = BLK * k, BLK * k + BLK
        S[:, 0:BLK] = A[lo:hi, lo:hi]
        S[:, BLK : 2 * BLK] = eye

        @pl.loop(0, BLK // 8)
        def _(g):
            panel(S, g)
            for at, hook in hooks.get(k, {}).items():
                pl.when(g == at)(hook)

        inverse = S[:, BLK : 2 * BLK]
        q = mm(X[:, lo:hi], inverse, 1, 1)
        Q[:, lo:hi] = q.astype(BF16)
        if k < blocks - 1:
            U = mm(inverse, A[lo:hi, hi:], 1, 0)
            A[hi:, hi:] = A[hi:, hi:] - mm(U, U, 0, 0)
            X[:, hi:] = X[:, hi:] - mm(q, U, 1, 0)


def scaled_update(first, second, g):
    new_first = 0.9 * first + 0.1 * g
    new_second = 0.999 * second + 0.001 * g * g
    scaled = 6.0 * (new_first / (1.0 - 0.9**10)) / (jnp.sqrt(new_second / (1.0 - 0.999**10)) + 1e-08)
    return scaled.astype(BF16)


def kernel(
    slots, bucket_of, grads, raw, first, second, basis_out, update_out, rows_out,
    X, A, S, Q, G, T, RA, RB, SA, SB, XS, XR, GS, MM, PR, U, GR, MT, GT,
    loc, ys, yr, tws, twr, mzs, mzr, mxs, mxr, rs, rr, xs, xr, gs, gr, es, er,
):
    dp, f = lax.axis_index("dp"), lax.axis_index("fsdp")
    z, xl, c = dp // 4, lax.rem(dp // 2, 2), lax.rem(dp, 2)
    xh, y = f // NY, lax.rem(f, NY)
    d = 1 - 2 * c

    def zat(k):
        return lax.rem(z + d * k + 2 * NZ, NZ)

    def at_z(k):
        return (zat(k) * 4 + xl * 2 + c, f)

    ahead, behind = at_z(1), at_z(-1)
    across = (z * 4 + (1 - xl) * 2 + c, f)
    twin = (z * 4 + xl * 2 + 1 - c, f)
    up, down = (dp, xh * NY + lax.rem(y + 1, NY)), (dp, xh * NY + lax.rem(y + NY - 1, NY))
    mirror = (z * 4 + (1 - xl) * 2 + c, (1 - xh) * NY + y)

    def remote(src, dst, send, recv, to):
        return pltpu.make_async_remote_copy(
            src_ref=src, dst_ref=dst, send_sem=send, recv_sem=recv,
            device_id=to, device_id_type=pl.DeviceIdType.MESH,
        )

    def fblock(h, yy, lo=0, n=128):
        return X.at[pl.ds(pl.multiple_of((h * NY + lax.rem(yy + 2 * NY, NY)) * 128 + lo, 64), n), :]

    def y_send(i):
        what = [
            (fblock(xh, y), up), (fblock(xh, y), down), (fblock(xh, y), mirror),
            (fblock(1 - xh, y), up), (fblock(1 - xh, y), down),
            (fblock(xh, y - 1, 0, 64), up), (fblock(xh, y + 1, 64, 64), down),
            (fblock(1 - xh, y - 1, 0, 64), up), (fblock(1 - xh, y + 1, 64, 64), down),
        ][i]
        return remote(what[0], what[0], ys.at[i], yr.at[i], what[1])

    def y_recv(i):
        what = [
            fblock(xh, y - 1), fblock(xh, y + 1), fblock(1 - xh, y),
            fblock(1 - xh, y - 1), fblock(1 - xh, y + 1),
            fblock(xh, y - 2, 0, 64), fblock(xh, y + 2, 64, 64),
            fblock(1 - xh, y - 2, 0, 64), fblock(1 - xh, y + 2, 64, 64),
        ][i]
        remote(what, what, ys.at[i], yr.at[i], up).wait_recv()

    def mblock(k, h):
        return MM.at[pl.ds(pl.multiple_of(zat(k) * 16 + h * 8, 8), 8)]

    def mz(s, way, k):
        i = s if way > 0 else 4 + s
        return remote(mblock(k, xl), mblock(k, xl), mzs.at[i], mzr.at[i], ahead if way > 0 else behind)

    def mx(i, k):
        return remote(mblock(k, xl), mblock(k, xl), mxs.at[i], mxr.at[i], across)

    def mx_recv(i, k):
        remote(mblock(k, 1 - xl), mblock(k, 1 - xl), mxs.at[i], mxr.at[i], across).wait_recv()

    def m_start():
        mz(0, 1, 0).start()
        mz(0, -1, 0).start()
        mx(0, 0).start()

    def m_step(s):
        mz(s - 1, 1, -s).wait_recv()
        if s < 4:
            mz(s, 1, -s).start()
        mx(s, -s).start()
        if s < 4:
            mz(s - 1, -1, s).wait_recv()
            if s < 3:
                mz(s, -1, s).start()
            mx(4 + s, s).start()

    def own(k):
        rows = pl.ds(pl.multiple_of(zat(k) * 128, 128), 128)
        return G[rows, :].astype(F32) + T[rows, :].astype(F32)

    def ra(s):
        return remote(SA if s == 0 else RA.at[s - 1], RA.at[s], rs.at[s], rr.at[s], ahead)

    def rb(s):
        return remote(SB if s == 0 else RB.at[s - 1], RB.at[s], rs.at[4 + s], rr.at[4 + s], behind)

    def r_start():
        SA[...] = own(4).astype(BF16)
        ra(0).start()
        SB[...] = own(-3).astype(BF16)
        rb(0).start()

    def r_step(s):
        ra(s - 1).wait_recv()
        RA[s - 1] = (RA[s - 1].astype(F32) + own(4 - s)).astype(BF16)
        ra(s).start()
        if s < 3:
            rb(s - 1).wait_recv()
            RB[s - 1] = (RB[s - 1].astype(F32) + own(s - 3)).astype(BF16)
            rb(s).start()

    x_sum = remote(XS, XR, xs, xr, across)

    def r_last():
        ra(3).wait_recv()
        rb(2).wait_recv()
        XS[...] = (own(0) + (RA[3].astype(F32) + RB[2].astype(F32))).astype(BF16)
        x_sum.start()

    def gblock(k):
        return GS.at[pl.ds(pl.multiple_of(zat(k) * 128, 128), 128), :]

    def gz(s, way, k):
        i = s if way > 0 else 4 + s
        return remote(gblock(k), gblock(k), gs.at[i], gr.at[i], ahead if way > 0 else behind)

    def g_start():
        x_sum.wait_recv()
        GS[pl.ds(pl.multiple_of(z * 128, 128), 128), :] = (
            XS[...].astype(F32) + XR[...].astype(F32)
        ).astype(BF16)
        gz(0, 1, 0).start()
        gz(0, -1, 0).start()

    def g_step(s):
        gz(s - 1, 1, -s).wait_recv()
        if s < 4:
            gz(s, 1, -s).start()
            gz(s - 1, -1, s).wait_recv()
            if s < 3:
                gz(s, -1, s).start()

    partners = (ahead, behind, across, twin, up, down, mirror)
    barrier = pltpu.get_barrier_semaphore()
    for to in partners:
        pl.semaphore_signal(barrier, inc=1, device_id=to, device_id_type=pl.DeviceIdType.MESH)
    own_raw = pltpu.make_async_copy(raw.at[c], fblock(xh, y), loc.at[0])
    own_grads = pltpu.make_async_copy(grads.at[0, c], G, loc.at[1])
    own_raw.start()
    own_grads.start()
    mine = pl.ds(pl.multiple_of(dp * CAP, CAP), CAP)
    MM[mine, 0] = first[c, 0].astype(BF16)
    MM[mine, 1] = second[c, 0].astype(BF16)
    MT[:, 0] = first[1 - c, 0].astype(BF16)
    MT[:, 1] = second[1 - c, 0].astype(BF16)
    own_raw.wait()
    pl.semaphore_wait(barrier, len(partners))

    for i in range(3):
        y_send(i).start()
    t_moments = remote(MT, MM.at[mine], tws.at[0], twr.at[0], twin)
    t_moments.start()
    t_grads = remote(grads.at[0, 1 - c], T, tws.at[1], twr.at[1], twin)
    t_grads.start()
    theirs = MM.at[pl.ds(pl.multiple_of((dp + 1 - 2 * c) * CAP, CAP), CAP)]
    own_grads.wait()
    t_grads.wait_recv()
    r_start()
    remote(MT, theirs, tws.at[0], twr.at[0], twin).wait_recv()
    m_start()

    y_recv(2)
    y_send(3).start()
    y_send(4).start()

    def gram(h, yy):
        part = fblock(h, yy)[...]
        return mm(part, part, 0, 0)

    A[...] = gram(xh, y) + gram(1 - xh, y)
    y_recv(0)
    y_send(5).start()
    y_recv(1)
    y_send(6).start()
    A[...] = A[...] + (gram(xh, y - 1) + gram(xh, y + 1))
    r_step(1)
    y_recv(3)
    y_send(7).start()
    y_recv(4)
    y_send(8).start()
    A[...] = A[...] + (gram(1 - xh, y - 1) + gram(1 - xh, y + 1))
    m_step(1)
    for i in range(5, 9):
        y_recv(i)
    A[...] = A[...] + (gram(xh, y + 2) + gram(1 - xh, y + 2))
    for i in range(9):
        y_send(i).wait_send()

    hooks = {
        0: {3: lambda: r_step(2), 8: lambda: m_step(2), 14: lambda: r_step(3)},
        1: {3: lambda: m_step(3), 8: r_last, 12: g_start, 15: lambda: m_step(4)},
        2: {6: lambda: g_step(1), 14: lambda: g_step(2)},
        3: {6: lambda: g_step(3)},
    }
    factor(A, X, S, Q, hooks)

    b_own = pltpu.make_async_copy(Q, basis_out.at[c], loc.at[2])
    b_twin = remote(Q, basis_out.at[c], es.at[0], er.at[0], twin)
    b_own.start()
    b_twin.start()
    g_step(4)
    for i in range(8):
        mx_recv(i, -i if i <= 4 else i - 4)

    pieces, height = 4, 256

    def u_own(i):
        part = pl.ds(i * height, height)
        return pltpu.make_async_copy(U.at[part, :], update_out.at[c, part, :], loc.at[3 + i])

    def u_twin(i):
        part = pl.ds(i * height, height)
        return remote(U.at[part, :], update_out.at[c, part, :], es.at[1 + i], er.at[1 + i], twin)

    for i in range(pieces):
        part, count = pl.ds(i * height, height), height // ROWS
        PR[i * count : (i + 1) * count] = mm(GS[part, :], Q[...], 1, 0, None).reshape(
            count, ROWS, PR.shape[2]
        )

        @pl.loop(i * count, (i + 1) * count)
        def _(b):
            rows = pl.ds(pl.multiple_of(b * ROWS, ROWS), ROWS)
            moments = MM[slots[c, b]]
            U[rows, :] = scaled_update(moments[0].astype(F32), moments[1].astype(F32), PR[b])

        u_own(i).start()
        u_twin(i).start()

    for i in range(CAP):
        GR[i] = PR[bucket_of[c, dp * CAP + i]]
        GT[i] = PR[bucket_of[c, (dp + 1 - 2 * c) * CAP + i]]
    r_own = pltpu.make_async_copy(GR, rows_out.at[c], loc.at[7])
    r_twin = remote(GT, rows_out.at[c], es.at[5], er.at[5], twin)
    r_own.start()
    r_twin.start()

    b_own.wait()
    r_own.wait()
    for i in range(pieces):
        u_own(i).wait()
        u_twin(i).wait_send()
    b_twin.wait_send()
    r_twin.wait_send()
    other = 1 - c
    remote(Q, basis_out.at[other], es.at[0], er.at[0], twin).wait_recv()
    remote(GT, rows_out.at[other], es.at[5], er.at[5], twin).wait_recv()
    for i in range(pieces):
        part = pl.ds(i * height, height)
        remote(U.at[part, :], update_out.at[other, part, :], es.at[1 + i], er.at[1 + i], twin).wait_recv()
    t_moments.wait_send()
    t_grads.wait_send()
    x_sum.wait_send()
    for s in range(4):
        ra(s).wait_send()
        mz(s, 1, -s).wait_send()
        gz(s, 1, -s).wait_send()
    for s in range(3):
        rb(s).wait_send()
        mz(s, -1, s).wait_send()
        gz(s, -1, s).wait_send()
    for i in range(8):
        mx(i, -i if i <= 4 else i - 4).wait_send()


def shards(grads, raw_proj, bucket_owner, first_moment, second_moment):
    matrices, local_rows, features = grads.shape[1:]
    rank = raw_proj.shape[2]
    buckets = bucket_owner.shape[1]
    capacity = first_moment.shape[2]
    slot_total = lax.axis_size("dp") * capacity
    same = bucket_owner[:, :, None] == bucket_owner[:, None, :]
    earlier = jnp.arange(buckets)[None, :] < jnp.arange(buckets)[:, None]
    ranks = jnp.sum(jnp.logical_and(same, earlier).astype(jnp.int32), axis=-1)
    slots = bucket_owner * capacity + ranks
    matches = slots[:, None, :] == jnp.arange(slot_total, dtype=jnp.int32)[None, :, None]
    occupied = jnp.any(matches, axis=2)
    bucket_of = jnp.sum(
        matches.astype(jnp.int32) * jnp.arange(buckets, dtype=jnp.int32)[None, None, :], axis=2
    )
    smem = pl.BlockSpec(memory_space=pltpu.SMEM)
    vmem = pl.BlockSpec(memory_space=pltpu.VMEM)
    anywhere = pl.BlockSpec(memory_space=pl.ANY)
    piece = (local_rows // NZ, features)
    dma = pltpu.SemaphoreType.DMA
    basis, update, grad_rows = pl.pallas_call(
        kernel,
        out_shape=(
            jax.ShapeDtypeStruct((matrices, features, rank), BF16),
            jax.ShapeDtypeStruct((matrices, local_rows, rank), BF16),
            jax.ShapeDtypeStruct((matrices, capacity, ROWS, rank), F32),
        ),
        in_specs=[smem, smem, anywhere, anywhere, vmem, vmem],
        out_specs=(anywhere, anywhere, anywhere),
        scratch_shapes=[
            pltpu.VMEM((features, rank), F32),
            pltpu.VMEM((rank, rank), F32),
            pltpu.VMEM((BLK, 2 * BLK), F32),
            pltpu.VMEM((features, rank), BF16),
            pltpu.VMEM((local_rows, features), BF16),
            pltpu.VMEM((local_rows, features), BF16),
            pltpu.VMEM((4, *piece), BF16),
            pltpu.VMEM((3, *piece), BF16),
            pltpu.VMEM(piece, BF16),
            pltpu.VMEM(piece, BF16),
            pltpu.VMEM(piece, BF16),
            pltpu.VMEM(piece, BF16),
            pltpu.VMEM((local_rows, features), BF16),
            pltpu.VMEM((slot_total, 2, ROWS, rank), BF16),
            pltpu.VMEM((buckets, ROWS, rank), F32),
            pltpu.VMEM((local_rows, rank), BF16),
            pltpu.VMEM((capacity, ROWS, rank), F32),
            pltpu.VMEM((capacity, 2, ROWS, rank), BF16),
            pltpu.VMEM((capacity, ROWS, rank), F32),
            dma((8,)), dma((9,)), dma((9,)), dma((2,)), dma((2,)),
            dma((7,)), dma((7,)), dma((8,)), dma((8,)), dma((7,)), dma((7,)),
            dma, dma, dma((7,)), dma((7,)), dma((6,)), dma((6,)),
        ],
        compiler_params=pltpu.CompilerParams(
            collective_id=0, has_side_effects=True, vmem_limit_bytes=52 << 20
        ),
        cost_estimate=pl.CostEstimate(
            flops=10_000_000_000, bytes_accessed=16_000_000, transcendentals=1_000_000
        ),
    )(slots, bucket_of, grads, raw_proj, first_moment, second_moment)
    start = lax.axis_index("dp") * capacity
    keep = lax.dynamic_slice_in_dim(occupied, start, capacity, 1)[:, :, None, None]
    first, second = first_moment[:, 0], second_moment[:, 0]
    first_out = jnp.where(keep, 0.9 * first + 0.1 * grad_rows, first)[:, None]
    second_out = jnp.where(keep, 0.999 * second + 0.001 * grad_rows * grad_rows, second)[:, None]
    weight_delta = jnp.einsum(
        "mdr,mkr->mdk", update, basis, preferred_element_type=F32
    ).astype(BF16)
    return (weight_delta, first_out, second_out)


def solution(mesh):
    return jax.shard_map(
        shards,
        mesh=mesh,
        in_specs=(
            P("dp", None, "fsdp", None),
            P(None, "fsdp", None),
            P(None, "fsdp"),
            P(None, "fsdp", "dp", None, None),
            P(None, "fsdp", "dp", None, None),
        ),
        out_specs=(
            P(None, "fsdp", None),
            P(None, "fsdp", "dp", None, None),
            P(None, "fsdp", "dp", None, None),
        ),
        check_vma=False,
    )
```

time: 796 us -> 118 us (0.15); the launches traced: 785 us -> 118 us
  waiting for transfers between devices: 467 us -> 0 us
  other arithmetic: 243 us -> 2.75 us
  Pallas kernels: 0 us -> 105 us
  local copies, waits for them, and re-layouts: 35 us -> 3.02 us
  matrix products: 26 us -> 6.61 us
  between operations: 14.5 us -> 0.67 us
    psum x2 -> x0, waiting for transfers between devices: 332 us -> none  [the longest x1 236 us: shards(): totals = lax.psum(blocks, 'dp')]
    another operation x21 -> x0, other arithmetic: 236 us -> none  [the longest x16 154 us: shards(): factor = jnp.linalg.cholesky(gram)]
    all_gather x2 -> x0, waiting for transfers between devices: 134 us -> none  [the longest x1 71.6 us: shards(): every_rows = lax.all_gather(owner_rows, 'dp', axis=1, tiled=True)]
    pallas_call x0 -> x1, Pallas kernels: none -> 105 us  [shards(): pl.pallas_call(kernel, out_shape=(jax.ShapeDtypeStruct((matrices, feature...]
    another operation x17 -> x0, local copies, waits for them, and re-layouts: 15.2 us -> none
    another operation x13 -> x0, matrix products: 13 us -> none  [the longest x6 6.73 us: shards(): factor = jnp.linalg.cholesky(gram)]
    gather x4 -> x0, local copies, waits for them, and re-layouts: 9.18 us -> none  [rows_at(): jnp.take(part_table, part_index, axis=0)]
  transfers between devices with their start and end apart: 4 -> 0, of which waited for: 4 -> 0; matrix products, arithmetic and copies ran while one was open for 0% -> 0% of each run, Pallas kernels for 0% -> 0%
where the time goes in v1:
time: 118 us
  Pallas kernels  105 us (89%)
  matrix products  6.61 us (6%)
  local copies, waits for them, and re-layouts  3.02 us (3%)
  other arithmetic  2.75 us (2%)
    pallas_call x1, Pallas kernels, shards(): pl.pallas_call(kernel, out_shape=(jax.ShapeDtypeStruct((matrices, feature...  105 us
    dot_general x1, matrix products, shards(): jnp.einsum('mdr,mkr->mdk', update, basis, preferred_element_type=F32)  6.61 us
    unnamed x6, local copies, waits for them, and re-layouts  2.94 us

profile of v1, /device:TPU:1, one launch (start us, length us, event | category | flops | bytes accessed | tf_op | source)
XLA Modules:
  0.0 117.9 jit_solution(7374120768849797136)
XLA Ops:
  0.7 0.9 convert_reduce_fusion
  1.6 0.7 multiply_add_fusion.slots
  2.3 0.1 fusion.5
  2.4 0.1 constant_dynamic-slice_fusion
  2.5 0.1 select_reduce_fusion.bucket_of
  2.6 0.0 copy-start
  2.6 0.9 copy-done
  3.5 0.0 copy-start.1
  3.5 0.9 copy-done.1
  4.5 0.0 copy-start.2
  4.5 1.0 copy-done.2
  5.5 104.9 %shard_map.76 = (bf16[2,1024,512]{2,1,0:T(8,128)(2,1)}, bf16[2,1024,512]{2,1,0:T(8,128)(2,1)}, f32[2,4,16,512]{3,2,1,0:T(8,128)S(1)}) custom-call(s32[2,64]{1,0:T(2,128)S(1)} %multiply_add_fusion.slots, s32[2,128]{1,0:T(2,128)S(1)} %select_reduce_fusion.bucket_of, bf16[1,2,1024,1024]{3,2,1,0:T(8,128)(2,1)} %grads.1, f32[2,128,512]{2,1,0:T(8,128)S(1)} %copy-done.2, ...), custom_call_target="tpu_custom_call" | custom-call | flops 10000000000 | bytes 16000000 | tf_op jit(solution)/shard_map/pallas_call | solution.py:366
  110.4 6.6 %convolution_convert_fusion = bf16[2,1024,1024]{2,1,0:T(8,128)(2,1)} fusion(bf16[2,1024,512]{2,1,0:T(8,128)(2,1)} %get-tuple-element.6, bf16[2,1024,512]{2,1,0:T(8,128)(2,1)} %get-tuple-element.7), kind=kOutput, calls=%fused_computation | convolution fusion | flops 2149580800 | bytes 8388608 | tf_op jit(solution)/shard_map/mdr,mkr->mdk/dot_general | solution.py:411
  117.0 0.9 fusion.2
  (1 shorter events, 0.0 us)
Async XLA Ops:
  2.6 1.0 copy-start
  3.5 0.9 copy-start.1
  4.5 1.0 copy-start.2

commit v2 on v1

--- a/solution.py
+++ b/solution.py
@@ -9,6 +9,7 @@
 F32 = jnp.float32
 BF16 = jnp.bfloat16
 BLK = 128
+PAN = 16
 NZ, NY, CAP, ROWS = 8, 4, 4, 16
 
 
@@ -18,29 +19,44 @@
     )
 
 
+def split(x):
+    high = x.astype(BF16).astype(F32)
+    middle = (x - high).astype(BF16).astype(F32)
+    return high, middle, (x - high) - middle
+
+
+def mm3(a, b, ca, cb):
+    ah, bh = a.astype(BF16), b.astype(BF16)
+    al, bl = (a - ah.astype(F32)).astype(BF16), (b - bh.astype(F32)).astype(BF16)
+    return mm(ah, bh, ca, cb, None) + (mm(ah, bl, ca, cb, None) + mm(al, bh, ca, cb, None))
+
+
 def panel(S, g):
-    rows = pl.ds(pl.multiple_of(8 * g, 8), 8)
+    rows = pl.ds(pl.multiple_of(PAN * g, PAN), PAN)
     V, W = S[rows, 0:BLK], S[rows, BLK : 2 * BLK]
-    turned = pltpu.roll(V, lax.rem(BLK - 8 * g, BLK), 1)
-    C = [jnp.broadcast_to(turned[:, k : k + 1], (8, BLK)) for k in range(8)]
-    sub = lax.broadcasted_iota(jnp.int32, (8, BLK), 0)
-    lane = lax.broadcasted_iota(jnp.int32, (8, BLK), 1)
-    pivot = jnp.ones((8, BLK), F32)
-    for j in range(8):
-        p = jnp.broadcast_to(C[j][j : j + 1, :], (8, BLK))
-        pivot = jnp.where(sub == j, p, pivot)
-        if j < 7:
-            m = jnp.where(sub > j, C[j] * (1.0 / p), 0.0)
-            for k in range(j + 1, 8):
-                C[k] = C[k] - m * jnp.broadcast_to(C[k][j : j + 1, :], (8, BLK))
-            V = V - m * jnp.broadcast_to(V[j : j + 1, :], (8, BLK))
-            W = W - m * jnp.broadcast_to(W[j : j + 1, :], (8, BLK))
+    turned = pltpu.roll(V, lax.rem(BLK - PAN * g, BLK), 1)
+    C = [jnp.broadcast_to(turned[:, k : k + 1], (PAN, BLK)) for k in range(PAN)]
+    sub = lax.broadcasted_iota(jnp.int32, (PAN, BLK), 0)
+    lane = lax.broadcasted_iota(jnp.int32, (PAN, BLK), 1)
+    pivot = jnp.ones((PAN, BLK), F32)
+    for j in range(PAN):
+        p = C[j][j : j + 1, :]
+        pivot = jnp.where(sub == j, jnp.broadcast_to(p, (PAN, BLK)), pivot)
+        if j < PAN - 1:
+            m = jnp.where(sub > j, C[j] * jnp.broadcast_to(1.0 / p, (PAN, BLK)), 0.0)
+            for k in range(j + 1, PAN):
+                C[k] = C[k] - m * jnp.broadcast_to(C[k][j : j + 1, :], (PAN, BLK))
+            V = V - m * jnp.broadcast_to(V[j : j + 1, :], (PAN, BLK))
+            W = W - m * jnp.broadcast_to(W[j : j + 1, :], (PAN, BLK))
     s = lax.rsqrt(pivot)
     s = s * (1.5 - 0.5 * pivot * s * s)
     VW = jnp.concatenate([V * s, W * s], axis=1)
     S[rows, :] = VW
-    later = jnp.where(lane >= 8 * g + 8, VW[:, 0:BLK], 0.0)
-    S[...] = S[...] - mm(later, VW, 0, 0)
+    high, middle, low = split(VW)
+    h, m, l = (jnp.where(lane >= PAN * (g + 1), x[:, 0:BLK], 0.0) for x in (high, middle, low))
+    left = jnp.concatenate([h, h, m, h, l, m], axis=0).astype(BF16)
+    right = jnp.concatenate([high, middle, high, low, high, middle], axis=0).astype(BF16)
+    S[...] = S[...] - mm(left, right, 0, 0, None)
 
 
 def factor(A, X, S, Q, hooks):
@@ -54,19 +70,19 @@
         S[:, 0:BLK] = A[lo:hi, lo:hi]
         S[:, BLK : 2 * BLK] = eye
 
-        @pl.loop(0, BLK // 8)
+        @pl.loop(0, BLK // PAN)
         def _(g):
             panel(S, g)
             for at, hook in hooks.get(k, {}).items():
                 pl.when(g == at)(hook)
 
         inverse = S[:, BLK : 2 * BLK]
-        q = mm(X[:, lo:hi], inverse, 1, 1)
+        q = mm3(X[:, lo:hi], inverse, 1, 1)
         Q[:, lo:hi] = q.astype(BF16)
         if k < blocks - 1:
             U = mm(inverse, A[lo:hi, hi:], 1, 0)
             A[hi:, hi:] = A[hi:, hi:] - mm(U, U, 0, 0)
-            X[:, hi:] = X[:, hi:] - mm(q, U, 1, 0)
+            X[:, hi:] = X[:, hi:] - mm3(q, U, 1, 0)
 
 
 def scaled_update(first, second, g):
@@ -78,8 +94,8 @@
 
 def kernel(
     slots, bucket_of, grads, raw, first, second, basis_out, update_out, rows_out,
-    X, A, S, Q, G, T, RA, RB, SA, SB, XS, XR, GS, MM, PR, U, GR, MT, GT,
-    loc, ys, yr, tws, twr, mzs, mzr, mxs, mxr, rs, rr, xs, xr, gs, gr, es, er,
+    X, A, S, Q, G, T, RA, RB, SA, SB, XS, XR, MM, MO, PB, U, GR, MT, GT,
+    loc, uo, us, ur, ys, yr, tws, twr, mzs, mzr, mxs, mxr, rs, rr, xs, xr, gs, gr, es, er,
 ):
     dp, f = lax.axis_index("dp"), lax.axis_index("fsdp")
     z, xl, c = dp // 4, lax.rem(dp // 2, 2), lax.rem(dp, 2)
@@ -181,24 +197,27 @@
 
     x_sum = remote(XS, XR, xs, xr, across)
 
+    def r_sum():
+        x_sum.wait_recv()
+        x_sum.wait_send()
+        XS[...] = (XS[...].astype(F32) + XR[...].astype(F32)).astype(BF16)
+
     def r_last():
         ra(3).wait_recv()
         rb(2).wait_recv()
         XS[...] = (own(0) + (RA[3].astype(F32) + RB[2].astype(F32))).astype(BF16)
         x_sum.start()
 
-    def gblock(k):
-        return GS.at[pl.ds(pl.multiple_of(zat(k) * 128, 128), 128), :]
+    def pblock(k):
+        return PB.at[pl.ds(pl.multiple_of(zat(k) * 8, 8), 8)]
 
     def gz(s, way, k):
         i = s if way > 0 else 4 + s
-        return remote(gblock(k), gblock(k), gs.at[i], gr.at[i], ahead if way > 0 else behind)
+        return remote(pblock(k), pblock(k), gs.at[i], gr.at[i], ahead if way > 0 else behind)
 
     def g_start():
-        x_sum.wait_recv()
-        GS[pl.ds(pl.multiple_of(z * 128, 128), 128), :] = (
-            XS[...].astype(F32) + XR[...].astype(F32)
-        ).astype(BF16)
+        part = mm(XS[...], Q[...], 1, 0, None)
+        pblock(0)[...] = part.reshape(8, ROWS, part.shape[1]).astype(BF16)
         gz(0, 1, 0).start()
         gz(0, -1, 0).start()
 
@@ -218,11 +237,16 @@
     own_grads = pltpu.make_async_copy(grads.at[0, c], G, loc.at[1])
     own_raw.start()
     own_grads.start()
+    own_moments = [
+        pltpu.make_async_copy(ref, MO.at[i], loc.at[2 + i]) for i, ref in enumerate((first, second))
+    ]
+    for copy in own_moments:
+        copy.start()
     mine = pl.ds(pl.multiple_of(dp * CAP, CAP), CAP)
-    MM[mine, 0] = first[c, 0].astype(BF16)
-    MM[mine, 1] = second[c, 0].astype(BF16)
-    MT[:, 0] = first[1 - c, 0].astype(BF16)
-    MT[:, 1] = second[1 - c, 0].astype(BF16)
+    for i, copy in enumerate(own_moments):
+        copy.wait()
+        MM[mine, i] = MO[i, c, 0].astype(BF16)
+        MT[:, i] = MO[i, 1 - c, 0].astype(BF16)
     own_raw.wait()
     pl.semaphore_wait(barrier, len(partners))
 
@@ -267,70 +291,73 @@
         y_send(i).wait_send()
 
     hooks = {
-        0: {3: lambda: r_step(2), 8: lambda: m_step(2), 14: lambda: r_step(3)},
-        1: {3: lambda: m_step(3), 8: r_last, 12: g_start, 15: lambda: m_step(4)},
-        2: {6: lambda: g_step(1), 14: lambda: g_step(2)},
-        3: {6: lambda: g_step(3)},
+        0: {2: lambda: r_step(2), 6: lambda: m_step(2)},
+        1: {2: lambda: r_step(3), 6: lambda: m_step(3)},
+        2: {5: r_last},
+        3: {2: lambda: m_step(4), 6: r_sum},
     }
     factor(A, X, S, Q, hooks)
-
-    b_own = pltpu.make_async_copy(Q, basis_out.at[c], loc.at[2])
+    g_start()
+
+    b_own = pltpu.make_async_copy(Q, basis_out.at[c], loc.at[4])
     b_twin = remote(Q, basis_out.at[c], es.at[0], er.at[0], twin)
     b_own.start()
     b_twin.start()
-    g_step(4)
     for i in range(8):
         mx_recv(i, -i if i <= 4 else i - 4)
 
-    pieces, height = 4, 256
-
-    def u_own(i):
-        part = pl.ds(i * height, height)
-        return pltpu.make_async_copy(U.at[part, :], update_out.at[c, part, :], loc.at[3 + i])
-
-    def u_twin(i):
-        part = pl.ds(i * height, height)
-        return remote(U.at[part, :], update_out.at[c, part, :], es.at[1 + i], er.at[1 + i], twin)
-
-    for i in range(pieces):
-        part, count = pl.ds(i * height, height), height // ROWS
-        PR[i * count : (i + 1) * count] = mm(GS[part, :], Q[...], 1, 0, None).reshape(
-            count, ROWS, PR.shape[2]
-        )
-
-        @pl.loop(i * count, (i + 1) * count)
-        def _(b):
-            rows = pl.ds(pl.multiple_of(b * ROWS, ROWS), ROWS)
+    def urows(k):
+        return pl.ds(pl.multiple_of(zat(k) * 128, 128), 128)
+
+    def u_own(i, k):
+        return pltpu.make_async_copy(U.at[urows(k), :], update_out.at[c, urows(k), :], uo.at[i])
+
+    def u_twin(i, k, at):
+        return remote(U.at[urows(k), :], update_out.at[at, urows(k), :], us.at[i], ur.at[i], twin)
+
+    def update(i, k):
+        @pl.loop(0, 8)
+        def _(j):
+            b = zat(k) * 8 + j
             moments = MM[slots[c, b]]
-            U[rows, :] = scaled_update(moments[0].astype(F32), moments[1].astype(F32), PR[b])
-
-        u_own(i).start()
-        u_twin(i).start()
+            U[pl.ds(pl.multiple_of(b * ROWS, ROWS), ROWS), :] = scaled_update(
+                moments[0].astype(F32), moments[1].astype(F32), PB[b].astype(F32)
+            )
+
+        u_own(i, k).start()
+        u_twin(i, k, c).start()
+
+    order = (0, -1, 1, -2, 2, -3, 3, 4)
+    update(0, 0)
+    for s in range(1, 4):
+        g_step(s)
+        update(2 * s - 1, -s)
+        update(2 * s, s)
+    g_step(4)
+    update(7, 4)
 
     for i in range(CAP):
-        GR[i] = PR[bucket_of[c, dp * CAP + i]]
-        GT[i] = PR[bucket_of[c, (dp + 1 - 2 * c) * CAP + i]]
-    r_own = pltpu.make_async_copy(GR, rows_out.at[c], loc.at[7])
-    r_twin = remote(GT, rows_out.at[c], es.at[5], er.at[5], twin)
+        GR[i] = PB[bucket_of[c, dp * CAP + i]].astype(F32)
+        GT[i] = PB[bucket_of[c, (dp + 1 - 2 * c) * CAP + i]].astype(F32)
+    r_own = pltpu.make_async_copy(GR, rows_out.at[c], loc.at[5])
+    r_twin = remote(GT, rows_out.at[c], es.at[1], er.at[1], twin)
     r_own.start()
     r_twin.start()
 
+    other = 1 - c
+    for i, k in enumerate(order):
+        u_own(i, k).wait()
+        u_twin(i, k, c).wait_send()
+    for i, k in enumerate(order):
+        u_twin(i, -k, other).wait_recv()
     b_own.wait()
     r_own.wait()
-    for i in range(pieces):
-        u_own(i).wait()
-        u_twin(i).wait_send()
     b_twin.wait_send()
     r_twin.wait_send()
-    other = 1 - c
     remote(Q, basis_out.at[other], es.at[0], er.at[0], twin).wait_recv()
-    remote(GT, rows_out.at[other], es.at[5], er.at[5], twin).wait_recv()
-    for i in range(pieces):
-        part = pl.ds(i * height, height)
-        remote(U.at[part, :], update_out.at[other, part, :], es.at[1 + i], er.at[1 + i], twin).wait_recv()
+    remote(GT, rows_out.at[other], es.at[1], er.at[1], twin).wait_recv()
     t_moments.wait_send()
     t_grads.wait_send()
-    x_sum.wait_send()
     for s in range(4):
         ra(s).wait_send()
         mz(s, 1, -s).wait_send()
@@ -341,6 +368,10 @@
         gz(s, -1, s).wait_send()
     for i in range(8):
         mx(i, -i if i <= 4 else i - 4).wait_send()
+
+
+def delta_kernel(update, basis, out):
+    out[0] = mm(update[0], basis[0], 1, 1, None).astype(BF16)
 
 
 def shards(grads, raw_proj, bucket_owner, first_moment, second_moment):
@@ -359,7 +390,6 @@
         matches.astype(jnp.int32) * jnp.arange(buckets, dtype=jnp.int32)[None, None, :], axis=2
     )
     smem = pl.BlockSpec(memory_space=pltpu.SMEM)
-    vmem = pl.BlockSpec(memory_space=pltpu.VMEM)
     anywhere = pl.BlockSpec(memory_space=pl.ANY)
     piece = (local_rows // NZ, features)
     dma = pltpu.SemaphoreType.DMA
@@ -370,7 +400,7 @@
             jax.ShapeDtypeStruct((matrices, local_rows, rank), BF16),
             jax.ShapeDtypeStruct((matrices, capacity, ROWS, rank), F32),
         ),
-        in_specs=[smem, smem, anywhere, anywhere, vmem, vmem],
+        in_specs=[smem, smem] + [anywhere] * 4,
         out_specs=(anywhere, anywhere, anywhere),
         scratch_shapes=[
             pltpu.VMEM((features, rank), F32),
@@ -385,19 +415,19 @@
             pltpu.VMEM(piece, BF16),
             pltpu.VMEM(piece, BF16),
             pltpu.VMEM(piece, BF16),
-            pltpu.VMEM((local_rows, features), BF16),
             pltpu.VMEM((slot_total, 2, ROWS, rank), BF16),
-            pltpu.VMEM((buckets, ROWS, rank), F32),
+            pltpu.VMEM((2, *first_moment.shape), F32),
+            pltpu.VMEM((buckets, ROWS, rank), BF16),
             pltpu.VMEM((local_rows, rank), BF16),
             pltpu.VMEM((capacity, ROWS, rank), F32),
             pltpu.VMEM((capacity, 2, ROWS, rank), BF16),
             pltpu.VMEM((capacity, ROWS, rank), F32),
-            dma((8,)), dma((9,)), dma((9,)), dma((2,)), dma((2,)),
+            dma((6,)), dma((8,)), dma((8,)), dma((8,)), dma((9,)), dma((9,)), dma((2,)), dma((2,)),
             dma((7,)), dma((7,)), dma((8,)), dma((8,)), dma((7,)), dma((7,)),
-            dma, dma, dma((7,)), dma((7,)), dma((6,)), dma((6,)),
+            dma, dma, dma((7,)), dma((7,)), dma((2,)), dma((2,)),
         ],
         compiler_params=pltpu.CompilerParams(
-            collective_id=0, has_side_effects=True, vmem_limit_bytes=52 << 20
+            collective_id=0, has_side_effects=True, vmem_limit_bytes=56 << 20
         ),
         cost_estimate=pl.CostEstimate(
             flops=10_000_000_000, bytes_accessed=16_000_000, transcendentals=1_000_000
@@ -408,9 +438,17 @@
     first, second = first_moment[:, 0], second_moment[:, 0]
     first_out = jnp.where(keep, 0.9 * first + 0.1 * grad_rows, first)[:, None]
     second_out = jnp.where(keep, 0.999 * second + 0.001 * grad_rows * grad_rows, second)[:, None]
-    weight_delta = jnp.einsum(
-        "mdr,mkr->mdk", update, basis, preferred_element_type=F32
-    ).astype(BF16)
+    height = 256
+    weight_delta = pl.pallas_call(
+        delta_kernel,
+        out_shape=jax.ShapeDtypeStruct((matrices, local_rows, features), BF16),
+        grid=(matrices, local_rows // height),
+        in_specs=[
+            pl.BlockSpec((1, height, rank), lambda m, i: (m, i, 0)),
+            pl.BlockSpec((1, features, rank), lambda m, i: (m, 0, 0)),
+        ],
+        out_specs=pl.BlockSpec((1, height, features), lambda m, i: (m, i, 0)),
+    )(update, basis)
     return (weight_delta, first_out, second_out)
 
 

time: 118 us -> 104 us (0.88)
  matrix products: 6.61 us -> 0 us
  Pallas kernels: 105 us -> 99.3 us
  local copies, waits for them, and re-layouts: 3.02 us -> 0.1 us
    pallas_call x1, Pallas kernels: 105 us -> 90.8 us  [shards(): pl.pallas_call(kernel, out_shape=(jax.ShapeDtypeStruct((matrices, feature...]
    pallas_call x0 -> x1, Pallas kernels: none -> 8.51 us  [shards(): pl.pallas_call(delta_kernel, out_shape=jax.ShapeDtypeStruct((matrices, lo...]
    dot_general x1 -> x0, matrix products: 6.61 us -> none  [shards(): jnp.einsum('mdr,mkr->mdk', update, basis, preferred_element_type=F32)]
    unnamed x6 -> x8, local copies, waits for them, and re-layouts: 2.94 us -> 0.02 us
where the time goes in v2:
time: 104 us; the launch traced here: 103 us
  Pallas kernels  99.3 us (95%)
  other arithmetic  3.31 us (3%)
    pallas_call x1, Pallas kernels, shards(): pl.pallas_call(kernel, out_shape=(jax.ShapeDtypeStruct((matrices, feature...  90.8 us
    pallas_call x1, Pallas kernels, shards(): pl.pallas_call(delta_kernel, out_shape=jax.ShapeDtypeStruct((matrices, lo...  8.51 us

profile of v2, /device:TPU:1, one launch (start us, length us, event | category | flops | bytes accessed | tf_op | source)
XLA Modules:
  0.0 103.4 jit_solution(5718526933870927287)
XLA Ops:
  0.7 0.9 convert_reduce_fusion
  1.6 0.7 multiply_add_fusion.slots
  2.3 0.0 copy-start.3
  2.3 0.1 fusion.5
  2.4 0.1 constant_dynamic-slice_fusion
  2.5 0.7 select_reduce_fusion.bucket_of
  3.1 0.0 copy-done.3
  3.1 90.8 %shard_map.76 = (bf16[2,1024,512]{2,1,0:T(8,128)(2,1)}, bf16[2,1024,512]{2,1,0:T(8,128)(2,1)}, f32[2,4,16,512]{3,2,1,0:T(8,128)}) custom-call(s32[2,64]{1,0:T(2,128)} %copy-done.3, s32[2,128]{1,0:T(2,128)} %select_reduce_fusion.bucket_of, bf16[1,2,1024,1024]{3,2,1,0:T(8,128)(2,1)} %grads.1, f32[2,128,512]{2,1,0:T(8,128)} %raw.1, ...), custom_call_target="tpu_custom_call" | custom-call | flops 10000000000 | bytes 16000000 | tf_op jit(solution)/shard_map/pallas_call | solution.py:396
  93.9 0.0 copy-start
  93.9 0.0 copy-start.1
  93.9 0.0 copy-start.2
  93.9 8.5 %shard_map.77 = bf16[2,1024,1024]{2,1,0:T(8,128)(2,1)} custom-call(bf16[2,1024,512]{2,1,0:T(8,128)(2,1)} %get-tuple-element.6.update, bf16[2,1024,512]{2,1,0:T(8,128)(2,1)} %get-tuple-element.7.basis), custom_call_target="tpu_custom_call" | custom-call | tf_op jit(solution)/shard_map/pallas_call | solution.py:442
  102.5 0.0 copy-done
  102.5 0.0 copy-done.1
  102.5 0.0 copy-done.2
  102.5 0.9 fusion.2
  (1 shorter events, 0.0 us)
Async XLA Ops:
  2.3 0.8 copy-start.3
  93.9 8.5 %copy-start = (f32[2,1,4,16,512]{4,3,2,1,0:T(8,128)S(1)}, f32[2,1,4,16,512]{4,3,2,1,0:T(8,128)}, u32[]{:S(2)}) copy-start(f32[2,1,4,16,512]{4,3,2,1,0:T(8,128)} %first.1) | copy-start | bytes 786436
  93.9 8.5 %copy-start.1 = (f32[2,1,4,16,512]{4,3,2,1,0:T(8,128)S(1)}, f32[2,1,4,16,512]{4,3,2,1,0:T(8,128)}, u32[]{:S(2)}) copy-start(f32[2,1,4,16,512]{4,3,2,1,0:T(8,128)} %second.1) | copy-start | bytes 786436
  93.9 8.5 %copy-start.2 = (f32[2,4,16,512]{3,2,1,0:T(8,128)S(1)}, f32[2,4,16,512]{3,2,1,0:T(8,128)}, u32[]{:S(2)}) copy-start(f32[2,4,16,512]{3,2,1,0:T(8,128)} %get-tuple-element.8) | copy-start | bytes 786436

commit v3 on v2

--- a/solution.py
+++ b/solution.py
@@ -93,9 +93,9 @@
 
 
 def kernel(
-    slots, bucket_of, grads, raw, first, second, basis_out, update_out, rows_out,
-    X, A, S, Q, G, T, RA, RB, SA, SB, XS, XR, MM, MO, PB, U, GR, MT, GT,
-    loc, uo, us, ur, ys, yr, tws, twr, mzs, mzr, mxs, mxr, rs, rr, xs, xr, gs, gr, es, er,
+    slots, bucket_of, grads, raw, first, second, delta_out, rows_out,
+    X, A, S, Q, QT, G, T, RA, RB, SA, SB, XS, XR, MM, MO, PB, U, D, GT, MT,
+    loc, do, ds, dr, us, ur, ys, yr, tws, twr, mzs, mzr, rs, rr, xs, xr, gs, gr, es, er,
 ):
     dp, f = lax.axis_index("dp"), lax.axis_index("fsdp")
     z, xl, c = dp // 4, lax.rem(dp // 2, 2), lax.rem(dp, 2)
@@ -111,6 +111,10 @@
     ahead, behind = at_z(1), at_z(-1)
     across = (z * 4 + (1 - xl) * 2 + c, f)
     twin = (z * 4 + xl * 2 + 1 - c, f)
+    diagonal = (z * 4 + (1 - xl) * 2 + 1 - c, f)
+    half = Q.shape[1] // 2
+    columns = pl.ds(pl.multiple_of(xl * half, half), half)
+    others = pl.ds(pl.multiple_of((1 - xl) * half, half), half)
     up, down = (dp, xh * NY + lax.rem(y + 1, NY)), (dp, xh * NY + lax.rem(y + NY - 1, NY))
     mirror = (z * 4 + (1 - xl) * 2 + c, (1 - xh) * NY + y)
 
@@ -141,34 +145,24 @@
         ][i]
         remote(what, what, ys.at[i], yr.at[i], up).wait_recv()
 
-    def mblock(k, h):
-        return MM.at[pl.ds(pl.multiple_of(zat(k) * 16 + h * 8, 8), 8)]
+    def mblock(k):
+        return MM.at[pl.ds(pl.multiple_of(zat(k) * 16, 16), 16)]
 
     def mz(s, way, k):
         i = s if way > 0 else 4 + s
-        return remote(mblock(k, xl), mblock(k, xl), mzs.at[i], mzr.at[i], ahead if way > 0 else behind)
-
-    def mx(i, k):
-        return remote(mblock(k, xl), mblock(k, xl), mxs.at[i], mxr.at[i], across)
-
-    def mx_recv(i, k):
-        remote(mblock(k, 1 - xl), mblock(k, 1 - xl), mxs.at[i], mxr.at[i], across).wait_recv()
+        return remote(mblock(k), mblock(k), mzs.at[i], mzr.at[i], ahead if way > 0 else behind)
 
     def m_start():
         mz(0, 1, 0).start()
         mz(0, -1, 0).start()
-        mx(0, 0).start()
 
     def m_step(s):
         mz(s - 1, 1, -s).wait_recv()
         if s < 4:
             mz(s, 1, -s).start()
-        mx(s, -s).start()
-        if s < 4:
             mz(s - 1, -1, s).wait_recv()
             if s < 3:
                 mz(s, -1, s).start()
-            mx(4 + s, s).start()
 
     def own(k):
         rows = pl.ds(pl.multiple_of(zat(k) * 128, 128), 128)
@@ -216,7 +210,7 @@
         return remote(pblock(k), pblock(k), gs.at[i], gr.at[i], ahead if way > 0 else behind)
 
     def g_start():
-        part = mm(XS[...], Q[...], 1, 0, None)
+        part = mm(XS[...], Q[:, columns], 1, 0, None)
         pblock(0)[...] = part.reshape(8, ROWS, part.shape[1]).astype(BF16)
         gz(0, 1, 0).start()
         gz(0, -1, 0).start()
@@ -229,7 +223,7 @@
             if s < 3:
                 gz(s, -1, s).start()
 
-    partners = (ahead, behind, across, twin, up, down, mirror)
+    partners = (ahead, behind, across, twin, diagonal, up, down, mirror)
     barrier = pltpu.get_barrier_semaphore()
     for to in partners:
         pl.semaphore_signal(barrier, inc=1, device_id=to, device_id_type=pl.DeviceIdType.MESH)
@@ -242,25 +236,35 @@
     ]
     for copy in own_moments:
         copy.start()
-    mine = pl.ds(pl.multiple_of(dp * CAP, CAP), CAP)
+    def place(h, k):
+        return MM.at[pl.ds(pl.multiple_of((z * 4 + h * 2 + k) * CAP, CAP), CAP)]
+
+    targets = ((twin, xl, 1 - c), (across, 1 - xl, c), (diagonal, 1 - xl, 1 - c))
+
+    def moments_to(i):
+        to, h, k = targets[i]
+        return remote(MT.at[i], place(xl, c), tws.at[1 + i], twr.at[1 + i], to)
+
     for i, copy in enumerate(own_moments):
         copy.wait()
-        MM[mine, i] = MO[i, c, 0].astype(BF16)
-        MT[:, i] = MO[i, 1 - c, 0].astype(BF16)
+        place(xl, c)[:, i] = MO[i, c, 0, :, :, columns].astype(BF16)
+        MT[0, :, i] = MO[i, 1 - c, 0, :, :, columns].astype(BF16)
+        MT[1, :, i] = MO[i, c, 0, :, :, others].astype(BF16)
+        MT[2, :, i] = MO[i, 1 - c, 0, :, :, others].astype(BF16)
     own_raw.wait()
     pl.semaphore_wait(barrier, len(partners))
 
     for i in range(3):
         y_send(i).start()
-    t_moments = remote(MT, MM.at[mine], tws.at[0], twr.at[0], twin)
-    t_moments.start()
-    t_grads = remote(grads.at[0, 1 - c], T, tws.at[1], twr.at[1], twin)
+    t_grads = remote(grads.at[0, 1 - c], T, tws.at[0], twr.at[0], twin)
     t_grads.start()
-    theirs = MM.at[pl.ds(pl.multiple_of((dp + 1 - 2 * c) * CAP, CAP), CAP)]
+    for i in range(3):
+        moments_to(i).start()
     own_grads.wait()
     t_grads.wait_recv()
     r_start()
-    remote(MT, theirs, tws.at[0], twr.at[0], twin).wait_recv()
+    for i, (to, h, k) in enumerate(targets):
+        remote(MT.at[i], place(h, k), tws.at[1 + i], twr.at[1 + i], to).wait_recv()
     m_start()
 
     y_recv(2)
@@ -299,33 +303,38 @@
     factor(A, X, S, Q, hooks)
     g_start()
 
-    b_own = pltpu.make_async_copy(Q, basis_out.at[c], loc.at[4])
-    b_twin = remote(Q, basis_out.at[c], es.at[0], er.at[0], twin)
-    b_own.start()
-    b_twin.start()
-    for i in range(8):
-        mx_recv(i, -i if i <= 4 else i - 4)
-
-    def urows(k):
+    for lo in range(0, Q.shape[1], BLK):
+        QT[lo : lo + BLK, :] = Q[:, lo : lo + BLK].T
+
+    def rows_of(k):
         return pl.ds(pl.multiple_of(zat(k) * 128, 128), 128)
 
-    def u_own(i, k):
-        return pltpu.make_async_copy(U.at[urows(k), :], update_out.at[c, urows(k), :], uo.at[i])
-
-    def u_twin(i, k, at):
-        return remote(U.at[urows(k), :], update_out.at[at, urows(k), :], us.at[i], ur.at[i], twin)
+    def u_across(i, k, part):
+        there = U.at[rows_of(k), part]
+        return remote(there, there, us.at[i], ur.at[i], across)
+
+    def d_own(i, k):
+        return pltpu.make_async_copy(D.at[rows_of(k), :], delta_out.at[c, rows_of(k), :], do.at[i])
+
+    def d_twin(i, k, at):
+        return remote(D.at[rows_of(k), :], delta_out.at[at, rows_of(k), :], ds.at[i], dr.at[i], twin)
 
     def update(i, k):
         @pl.loop(0, 8)
         def _(j):
             b = zat(k) * 8 + j
             moments = MM[slots[c, b]]
-            U[pl.ds(pl.multiple_of(b * ROWS, ROWS), ROWS), :] = scaled_update(
+            U[pl.ds(pl.multiple_of(b * ROWS, ROWS), ROWS), columns] = scaled_update(
                 moments[0].astype(F32), moments[1].astype(F32), PB[b].astype(F32)
             )
 
-        u_own(i, k).start()
-        u_twin(i, k, c).start()
+        u_across(i, k, columns).start()
+
+    def delta(i, k):
+        u_across(i, k, others).wait_recv()
+        D[rows_of(k), :] = mm(U[rows_of(k), :], QT[...], 1, 0, None).astype(BF16)
+        d_own(i, k).start()
+        d_twin(i, k, c).start()
 
     order = (0, -1, 1, -2, 2, -3, 3, 4)
     update(0, 0)
@@ -333,31 +342,42 @@
         g_step(s)
         update(2 * s - 1, -s)
         update(2 * s, s)
+        for i in range(max(2 * s - 3, 0), 2 * s - 1):
+            delta(i, order[i])
     g_step(4)
     update(7, 4)
 
-    for i in range(CAP):
-        GR[i] = PB[bucket_of[c, dp * CAP + i]].astype(F32)
-        GT[i] = PB[bucket_of[c, (dp + 1 - 2 * c) * CAP + i]].astype(F32)
-    r_own = pltpu.make_async_copy(GR, rows_out.at[c], loc.at[5])
-    r_twin = remote(GT, rows_out.at[c], es.at[1], er.at[1], twin)
+    holders = ((xl, c), (xl, 1 - c), (1 - xl, c), (1 - xl, 1 - c))
+    to_holders = (None, twin, across, diagonal)
+
+    def rows_to(n, matrix, part):
+        return remote(GT.at[n], rows_out.at[matrix, :, :, part], es.at[n - 1], er.at[n - 1], to_holders[n])
+
+    for n, (h, k) in enumerate(holders):
+        for i in range(CAP):
+            GT[n, i] = PB[bucket_of[c, (z * 4 + h * 2 + k) * CAP + i]]
+    r_own = pltpu.make_async_copy(GT.at[0], rows_out.at[c, :, :, columns], loc.at[4])
     r_own.start()
-    r_twin.start()
-
-    other = 1 - c
+    for n in range(1, 4):
+        rows_to(n, c, columns).start()
+    for i in range(5, 8):
+        delta(i, order[i])
+
     for i, k in enumerate(order):
-        u_own(i, k).wait()
-        u_twin(i, k, c).wait_send()
+        d_own(i, k).wait()
+        d_twin(i, k, c).wait_send()
+        u_across(i, k, columns).wait_send()
     for i, k in enumerate(order):
-        u_twin(i, -k, other).wait_recv()
-    b_own.wait()
+        d_twin(i, -k, 1 - c).wait_recv()
     r_own.wait()
-    b_twin.wait_send()
-    r_twin.wait_send()
-    remote(Q, basis_out.at[other], es.at[0], er.at[0], twin).wait_recv()
-    remote(GT, rows_out.at[other], es.at[1], er.at[1], twin).wait_recv()
-    t_moments.wait_send()
+    for n in range(1, 4):
+        rows_to(n, c, columns).wait_send()
+    rows_to(1, 1 - c, columns).wait_recv()
+    rows_to(2, c, others).wait_recv()
+    rows_to(3, 1 - c, others).wait_recv()
     t_grads.wait_send()
+    for i in range(3):
+        moments_to(i).wait_send()
     for s in range(4):
         ra(s).wait_send()
         mz(s, 1, -s).wait_send()
@@ -366,12 +386,6 @@
         rb(s).wait_send()
         mz(s, -1, s).wait_send()
         gz(s, -1, s).wait_send()
-    for i in range(8):
-        mx(i, -i if i <= 4 else i - 4).wait_send()
-
-
-def delta_kernel(update, basis, out):
-    out[0] = mm(update[0], basis[0], 1, 1, None).astype(BF16)
 
 
 def shards(grads, raw_proj, bucket_owner, first_moment, second_moment):
@@ -393,20 +407,20 @@
     anywhere = pl.BlockSpec(memory_space=pl.ANY)
     piece = (local_rows // NZ, features)
     dma = pltpu.SemaphoreType.DMA
-    basis, update, grad_rows = pl.pallas_call(
+    weight_delta, grad_rows = pl.pallas_call(
         kernel,
         out_shape=(
-            jax.ShapeDtypeStruct((matrices, features, rank), BF16),
-            jax.ShapeDtypeStruct((matrices, local_rows, rank), BF16),
-            jax.ShapeDtypeStruct((matrices, capacity, ROWS, rank), F32),
+            jax.ShapeDtypeStruct((matrices, local_rows, features), BF16),
+            jax.ShapeDtypeStruct((matrices, capacity, ROWS, rank), BF16),
         ),
         in_specs=[smem, smem] + [anywhere] * 4,
-        out_specs=(anywhere, anywhere, anywhere),
+        out_specs=(anywhere, anywhere),
         scratch_shapes=[
             pltpu.VMEM((features, rank), F32),
             pltpu.VMEM((rank, rank), F32),
             pltpu.VMEM((BLK, 2 * BLK), F32),
             pltpu.VMEM((features, rank), BF16),
+            pltpu.VMEM((rank, features), BF16),
             pltpu.VMEM((local_rows, features), BF16),
             pltpu.VMEM((local_rows, features), BF16),
             pltpu.VMEM((4, *piece), BF16),
@@ -415,16 +429,16 @@
             pltpu.VMEM(piece, BF16),
             pltpu.VMEM(piece, BF16),
             pltpu.VMEM(piece, BF16),
-            pltpu.VMEM((slot_total, 2, ROWS, rank), BF16),
+            pltpu.VMEM((slot_total, 2, ROWS, rank // 2), BF16),
             pltpu.VMEM((2, *first_moment.shape), F32),
-            pltpu.VMEM((buckets, ROWS, rank), BF16),
+            pltpu.VMEM((buckets, ROWS, rank // 2), BF16),
             pltpu.VMEM((local_rows, rank), BF16),
-            pltpu.VMEM((capacity, ROWS, rank), F32),
-            pltpu.VMEM((capacity, 2, ROWS, rank), BF16),
-            pltpu.VMEM((capacity, ROWS, rank), F32),
-            dma((6,)), dma((8,)), dma((8,)), dma((8,)), dma((9,)), dma((9,)), dma((2,)), dma((2,)),
-            dma((7,)), dma((7,)), dma((8,)), dma((8,)), dma((7,)), dma((7,)),
-            dma, dma, dma((7,)), dma((7,)), dma((2,)), dma((2,)),
+            pltpu.VMEM((local_rows, features), BF16),
+            pltpu.VMEM((4, capacity, ROWS, rank // 2), BF16),
+            pltpu.VMEM((3, capacity, 2, ROWS, rank // 2), BF16),
+            dma((5,)), dma((8,)), dma((8,)), dma((8,)), dma((8,)), dma((8,)),
+            dma((9,)), dma((9,)), dma((4,)), dma((4,)), dma((7,)), dma((7,)),
+            dma((7,)), dma((7,)), dma, dma, dma((7,)), dma((7,)), dma((3,)), dma((3,)),
         ],
         compiler_params=pltpu.CompilerParams(
             collective_id=0, has_side_effects=True, vmem_limit_bytes=56 << 20
@@ -436,19 +450,9 @@
     start = lax.axis_index("dp") * capacity
     keep = lax.dynamic_slice_in_dim(occupied, start, capacity, 1)[:, :, None, None]
     first, second = first_moment[:, 0], second_moment[:, 0]
+    grad_rows = grad_rows.astype(F32)
     first_out = jnp.where(keep, 0.9 * first + 0.1 * grad_rows, first)[:, None]
     second_out = jnp.where(keep, 0.999 * second + 0.001 * grad_rows * grad_rows, second)[:, None]
-    height = 256
-    weight_delta = pl.pallas_call(
-        delta_kernel,
-        out_shape=jax.ShapeDtypeStruct((matrices, local_rows, features), BF16),
-        grid=(matrices, local_rows // height),
-        in_specs=[
-            pl.BlockSpec((1, height, rank), lambda m, i: (m, i, 0)),
-            pl.BlockSpec((1, features, rank), lambda m, i: (m, 0, 0)),
-        ],
-        out_specs=pl.BlockSpec((1, height, features), lambda m, i: (m, i, 0)),
-    )(update, basis)
     return (weight_delta, first_out, second_out)
 
 

time: 104 us -> 95.1 us (0.914)
  Pallas kernels: 99.3 us -> 85.3 us
  local copies, waits for them, and re-layouts: 0.1 us -> 4.73 us
    pallas_call x2 -> x1, Pallas kernels: 99.3 us -> 85.3 us  [shards(): pl.pallas_call(kernel, out_shape=(jax.ShapeDtypeStruct((matrices, local_r...]
    unnamed x8 -> x7, local copies, waits for them, and re-layouts: 0.02 us -> 4.65 us
where the time goes in v3:
time: 95.1 us; the launch traced here: 94.9 us
  Pallas kernels  85.3 us (90%)
  local copies, waits for them, and re-layouts  4.73 us (5%)
  other arithmetic  4.21 us (4%)
    pallas_call x1, Pallas kernels, shards(): pl.pallas_call(kernel, out_shape=(jax.ShapeDtypeStruct((matrices, local_r...  85.3 us
    unnamed x7, local copies, waits for them, and re-layouts  4.65 us

profile of v3, /device:TPU:1, one launch (start us, length us, event | category | flops | bytes accessed | tf_op | source)
XLA Modules:
  0.0 94.9 jit_solution(17029646890137277754)
XLA Ops:
  0.7 0.9 convert_reduce_fusion
  1.6 0.7 multiply_add_fusion.slots
  2.3 0.0 copy-start.2
  2.3 0.1 fusion.6
  2.4 0.1 constant_dynamic-slice_fusion
  2.5 0.7 select_reduce_fusion.bucket_of
  3.1 0.0 copy-done.2
  3.1 0.0 copy-start
  3.1 0.0 copy-start.1
  3.1 85.3 %shard_map.76 = (bf16[2,1024,1024]{2,1,0:T(8,128)(2,1)}, bf16[2,4,16,512]{3,2,1,0:T(8,128)(2,1)}) custom-call(s32[2,64]{1,0:T(2,128)} %copy-done.2, s32[2,128]{1,0:T(2,128)} %select_reduce_fusion.bucket_of, bf16[1,2,1024,1024]{3,2,1,0:T(8,128)(2,1)} %grads.1, f32[2,128,512]{2,1,0:T(8,128)} %raw.1, f32[2,1,4,16,512]{4,3,2,1,0:T(8,128)} %first.1, ...), custom_call_target="tpu_custom_call" | custom-call | flops 10000000000 | bytes 16000000 | tf_op jit(solution)/shard_map/pallas_call | solution.py:410
  88.4 0.0 copy-done
  88.4 0.0 copy-done.1
  88.5 1.8 %fusion.5 = (f32[2,1,4,16,512]{4,3,2,1,0:T(8,128)}, f32[2,1,4,16,512]{4,3,2,1,0:T(8,128)}) fusion(bf16[2,4,16,512]{3,2,1,0:T(8,128)(2,1)} %get-tuple-element.6, f32[2,1,4,16,512]{4,3,2,1,0:T(8,128)S(1)} %copy-done.1, pred[2,4]{1,0:T(4,128)(4,1)S(1)} %constant_dynamic-slice_fusion, f32[2,1,4,16,512]{4,3,2,1,0:T(8,128)S(1)} %copy-done), kind=kLoop, calls=%fused_computation.7 | loop fusion | flops 655360 | bytes 1179656
  90.3 4.6 %copy.13 = bf16[2,1024,1024]{2,1,0:T(8,128)(2,1)} copy(bf16[2,1024,1024]{2,1,0:T(8,128)(2,1)} %get-tuple-element.18) | data formatting | bytes 8388608
  (1 shorter events, 0.0 us)
Async XLA Ops:
  2.3 0.8 copy-start.2
  3.1 85.3 %copy-start = (f32[2,1,4,16,512]{4,3,2,1,0:T(8,128)S(1)}, f32[2,1,4,16,512]{4,3,2,1,0:T(8,128)}, u32[]{:S(2)}) copy-start(f32[2,1,4,16,512]{4,3,2,1,0:T(8,128)} %first.1) | copy-start | bytes 786436
  3.1 85.3 %copy-start.1 = (f32[2,1,4,16,512]{4,3,2,1,0:T(8,128)S(1)}, f32[2,1,4,16,512]{4,3,2,1,0:T(8,128)}, u32[]{:S(2)}) copy-start(f32[2,1,4,16,512]{4,3,2,1,0:T(8,128)} %second.1) | copy-start | bytes 786436

commit v4 on v3

--- a/solution.py
+++ b/solution.py
@@ -94,8 +94,8 @@
 
 def kernel(
     slots, bucket_of, grads, raw, first, second, delta_out, rows_out,
-    X, A, S, Q, QT, G, T, RA, RB, SA, SB, XS, XR, MM, MO, PB, U, D, GT, MT,
-    loc, do, ds, dr, us, ur, ys, yr, tws, twr, mzs, mzr, rs, rr, xs, xr, gs, gr, es, er,
+    X, A, S, Q, QT, G, T, RA, RB, SA, SB, XS, XR, GS, MM, MO, PB, U, GT, MT,
+    loc, ds, dr, us, ur, ys, yr, tws, twr, mzs, mzr, rs, rr, xs, xr, gs, gr, es, er,
 ):
     dp, f = lax.axis_index("dp"), lax.axis_index("fsdp")
     z, xl, c = dp // 4, lax.rem(dp // 2, 2), lax.rem(dp, 2)
@@ -164,9 +164,24 @@
             if s < 3:
                 mz(s, -1, s).start()
 
+    pieces = (4, -3, 3, -2, 2, -1, 1, 0)
+
+    def two_cores(k, h):
+        rows = pl.ds(pl.multiple_of(zat(k) * 128 + h * 64, 64), 64)
+        return G[rows, :].astype(F32) + T[rows, :].astype(F32)
+
+    def x_piece(i):
+        return remote(XS.at[i], XR.at[i], xs.at[i], xr.at[i], across)
+
+    def x_start():
+        for i, k in enumerate(pieces):
+            XS[i] = two_cores(k, 1 - xl).astype(BF16)
+            x_piece(i).start()
+
     def own(k):
-        rows = pl.ds(pl.multiple_of(zat(k) * 128, 128), 128)
-        return G[rows, :].astype(F32) + T[rows, :].astype(F32)
+        i = pieces.index(k)
+        x_piece(i).wait_recv()
+        return two_cores(k, xl) + XR[i].astype(F32)
 
     def ra(s):
         return remote(SA if s == 0 else RA.at[s - 1], RA.at[s], rs.at[s], rr.at[s], ahead)
@@ -189,18 +204,21 @@
             RB[s - 1] = (RB[s - 1].astype(F32) + own(s - 3)).astype(BF16)
             rb(s).start()
 
-    x_sum = remote(XS, XR, xs, xr, across)
-
-    def r_sum():
-        x_sum.wait_recv()
-        x_sum.wait_send()
-        XS[...] = (XS[...].astype(F32) + XR[...].astype(F32)).astype(BF16)
+    def half_sum(h):
+        there = GS.at[pl.ds(pl.multiple_of(h * 64, 64), 64), :]
+        return remote(there, there, xs.at[8], xr.at[8], across)
 
     def r_last():
+        mine = own(0)
         ra(3).wait_recv()
         rb(2).wait_recv()
-        XS[...] = (own(0) + (RA[3].astype(F32) + RB[2].astype(F32))).astype(BF16)
-        x_sum.start()
+        GS[pl.ds(pl.multiple_of(xl * 64, 64), 64), :] = (
+            mine + (RA[3].astype(F32) + RB[2].astype(F32))
+        ).astype(BF16)
+        half_sum(xl).start()
+
+    def r_sum():
+        half_sum(1 - xl).wait_recv()
 
     def pblock(k):
         return PB.at[pl.ds(pl.multiple_of(zat(k) * 8, 8), 8)]
@@ -210,7 +228,7 @@
         return remote(pblock(k), pblock(k), gs.at[i], gr.at[i], ahead if way > 0 else behind)
 
     def g_start():
-        part = mm(XS[...], Q[:, columns], 1, 0, None)
+        part = mm(GS[...], Q[:, columns], 1, 0, None)
         pblock(0)[...] = part.reshape(8, ROWS, part.shape[1]).astype(BF16)
         gz(0, 1, 0).start()
         gz(0, -1, 0).start()
@@ -262,7 +280,7 @@
         moments_to(i).start()
     own_grads.wait()
     t_grads.wait_recv()
-    r_start()
+    x_start()
     for i, (to, h, k) in enumerate(targets):
         remote(MT.at[i], place(h, k), tws.at[1 + i], twr.at[1 + i], to).wait_recv()
     m_start()
@@ -276,12 +294,12 @@
         return mm(part, part, 0, 0)
 
     A[...] = gram(xh, y) + gram(1 - xh, y)
+    r_start()
     y_recv(0)
     y_send(5).start()
     y_recv(1)
     y_send(6).start()
     A[...] = A[...] + (gram(xh, y - 1) + gram(xh, y + 1))
-    r_step(1)
     y_recv(3)
     y_send(7).start()
     y_recv(4)
@@ -295,10 +313,10 @@
         y_send(i).wait_send()
 
     hooks = {
-        0: {2: lambda: r_step(2), 6: lambda: m_step(2)},
-        1: {2: lambda: r_step(3), 6: lambda: m_step(3)},
-        2: {5: r_last},
-        3: {2: lambda: m_step(4), 6: r_sum},
+        0: {0: lambda: r_step(1), 4: lambda: m_step(2), 7: lambda: r_step(2)},
+        1: {3: lambda: m_step(3), 6: lambda: r_step(3)},
+        2: {3: r_last, 6: lambda: m_step(4)},
+        3: {4: r_sum},
     }
     factor(A, X, S, Q, hooks)
     g_start()
@@ -313,11 +331,9 @@
         there = U.at[rows_of(k), part]
         return remote(there, there, us.at[i], ur.at[i], across)
 
-    def d_own(i, k):
-        return pltpu.make_async_copy(D.at[rows_of(k), :], delta_out.at[c, rows_of(k), :], do.at[i])
-
     def d_twin(i, k, at):
-        return remote(D.at[rows_of(k), :], delta_out.at[at, rows_of(k), :], ds.at[i], dr.at[i], twin)
+        there = delta_out.at[at, rows_of(k), :]
+        return remote(there, there, ds.at[i], dr.at[i], twin)
 
     def update(i, k):
         @pl.loop(0, 8)
@@ -332,8 +348,7 @@
 
     def delta(i, k):
         u_across(i, k, others).wait_recv()
-        D[rows_of(k), :] = mm(U[rows_of(k), :], QT[...], 1, 0, None).astype(BF16)
-        d_own(i, k).start()
+        delta_out[c, rows_of(k), :] = mm(U[rows_of(k), :], QT[...], 1, 0, None).astype(BF16)
         d_twin(i, k, c).start()
 
     order = (0, -1, 1, -2, 2, -3, 3, 4)
@@ -364,7 +379,6 @@
         delta(i, order[i])
 
     for i, k in enumerate(order):
-        d_own(i, k).wait()
         d_twin(i, k, c).wait_send()
         u_across(i, k, columns).wait_send()
     for i, k in enumerate(order):
@@ -376,6 +390,9 @@
     rows_to(2, c, others).wait_recv()
     rows_to(3, 1 - c, others).wait_recv()
     t_grads.wait_send()
+    half_sum(xl).wait_send()
+    for i in range(8):
+        x_piece(i).wait_send()
     for i in range(3):
         moments_to(i).wait_send()
     for s in range(4):
@@ -405,16 +422,16 @@
     )
     smem = pl.BlockSpec(memory_space=pltpu.SMEM)
     anywhere = pl.BlockSpec(memory_space=pl.ANY)
-    piece = (local_rows // NZ, features)
+    piece = (local_rows // NZ // 2, features)
     dma = pltpu.SemaphoreType.DMA
     weight_delta, grad_rows = pl.pallas_call(
         kernel,
         out_shape=(
-            jax.ShapeDtypeStruct((matrices, local_rows, features), BF16),
+            pltpu.VMEM((matrices, local_rows, features), BF16),
             jax.ShapeDtypeStruct((matrices, capacity, ROWS, rank), BF16),
         ),
         in_specs=[smem, smem] + [anywhere] * 4,
-        out_specs=(anywhere, anywhere),
+        out_specs=(pl.BlockSpec(memory_space=pltpu.VMEM), anywhere),
         scratch_shapes=[
             pltpu.VMEM((features, rank), F32),
             pltpu.VMEM((rank, rank), F32),
@@ -427,18 +444,18 @@
             pltpu.VMEM((3, *piece), BF16),
             pltpu.VMEM(piece, BF16),
             pltpu.VMEM(piece, BF16),
-            pltpu.VMEM(piece, BF16),
-            pltpu.VMEM(piece, BF16),
+            pltpu.VMEM((8, *piece), BF16),
+            pltpu.VMEM((8, *piece), BF16),
+            pltpu.VMEM((local_rows // NZ, features), BF16),
             pltpu.VMEM((slot_total, 2, ROWS, rank // 2), BF16),
             pltpu.VMEM((2, *first_moment.shape), F32),
             pltpu.VMEM((buckets, ROWS, rank // 2), BF16),
             pltpu.VMEM((local_rows, rank), BF16),
-            pltpu.VMEM((local_rows, features), BF16),
             pltpu.VMEM((4, capacity, ROWS, rank // 2), BF16),
             pltpu.VMEM((3, capacity, 2, ROWS, rank // 2), BF16),
-            dma((5,)), dma((8,)), dma((8,)), dma((8,)), dma((8,)), dma((8,)),
+            dma((5,)), dma((8,)), dma((8,)), dma((8,)), dma((8,)),
             dma((9,)), dma((9,)), dma((4,)), dma((4,)), dma((7,)), dma((7,)),
-            dma((7,)), dma((7,)), dma, dma, dma((7,)), dma((7,)), dma((3,)), dma((3,)),
+            dma((7,)), dma((7,)), dma((9,)), dma((9,)), dma((7,)), dma((7,)), dma((3,)), dma((3,)),
         ],
         compiler_params=pltpu.CompilerParams(
             collective_id=0, has_side_effects=True, vmem_limit_bytes=56 << 20

time: 95.1 us -> 86.4 us (0.909)
  Pallas kernels: 85.3 us -> 80.2 us
  local copies, waits for them, and re-layouts: 4.73 us -> 2.11 us
    pallas_call x1, Pallas kernels: 85.3 us -> 80.2 us  [shards(): pl.pallas_call(kernel, out_shape=(pltpu.VMEM((matrices, local_rows, featu...]
    unnamed x7 -> x9, local copies, waits for them, and re-layouts: 4.65 us -> 2.04 us
where the time goes in v4:
time: 86.4 us; the launch traced here: 86.3 us
  Pallas kernels  80.2 us (93%)
  other arithmetic  3.3 us (4%)
  local copies, waits for them, and re-layouts  2.11 us (2%)
    pallas_call x1, Pallas kernels, shards(): pl.pallas_call(kernel, out_shape=(pltpu.VMEM((matrices, local_rows, featu...  80.2 us
    unnamed x9, local copies, waits for them, and re-layouts  2.04 us

profile of v4, /device:TPU:1, one launch (start us, length us, event | category | flops | bytes accessed | tf_op | source)
XLA Modules:
  0.0 86.3 jit_solution(17293606477711471003)
XLA Ops:
  0.7 0.9 %convert_reduce_fusion = s32[2,64]{1,0:T(2,128)S(1)} fusion(s32[2,64]{1,0:T(2,128)} %param.7, pred[64,64]{1,0:T(8,128)(4,1)S(1)} %iota_compare_fusion.1), kind=kLoop, calls=%fused_computation.13 | loop fusion | flops 32640 | bytes 5120 | tf_op jit(solution)/shard_map/reduce_sum | solution.py:416
  1.6 0.7 multiply_add_fusion.slots
  2.3 0.0 copy-start.3
  2.3 0.1 fusion.6
  2.4 0.1 constant_dynamic-slice_fusion
  2.5 0.7 select_reduce_fusion.bucket_of
  3.1 0.0 copy-done.3
  3.1 80.2 %shard_map.76 = (bf16[2,1024,1024]{2,1,0:T(8,128)(2,1)S(1)}, bf16[2,4,16,512]{3,2,1,0:T(8,128)(2,1)}) custom-call(s32[2,64]{1,0:T(2,128)} %copy-done.3, s32[2,128]{1,0:T(2,128)} %select_reduce_fusion.bucket_of, bf16[1,2,1024,1024]{3,2,1,0:T(8,128)(2,1)} %grads.1, f32[2,128,512]{2,1,0:T(8,128)} %raw.1, f32[2,1,4,16,512]{4,3,2,1,0:T(8,128)} %first.1, ...), custom_call_target="tpu_custom_call" | custom-call | flops 10000000000 | bytes 16000000 | tf_op jit(solution)/shard_map/pallas_call | solution.py:427
  83.3 0.0 copy-start
  83.3 0.0 copy-start.1
  83.3 0.0 copy-start.2
  83.3 2.0 %copy.13 = bf16[2,1024,1024]{2,1,0:T(8,128)(2,1)} copy(bf16[2,1024,1024]{2,1,0:T(8,128)(2,1)S(1)} %get-tuple-element.15) | data formatting | bytes 8388608
  85.3 0.0 copy-done
  85.3 0.0 copy-done.1
  85.3 0.0 copy-done.2
  85.4 0.9 %fusion.5 = (f32[2,1,4,16,512]{4,3,2,1,0:T(8,128)}, f32[2,1,4,16,512]{4,3,2,1,0:T(8,128)}) fusion(bf16[2,4,16,512]{3,2,1,0:T(8,128)(2,1)S(1)} %copy-done.2, f32[2,1,4,16,512]{4,3,2,1,0:T(8,128)S(1)} %copy-done.1, pred[2,4]{1,0:T(4,128)(4,1)S(1)} %constant_dynamic-slice_fusion, f32[2,1,4,16,512]{4,3,2,1,0:T(8,128)S(1)} %copy-done), kind=kLoop, calls=%fused_computation.7 | loop fusion | flops 655360 | bytes 1179656
  (1 shorter events, 0.0 us)
Async XLA Ops:
  2.3 0.8 copy-start.3
  83.3 2.1 %copy-start = (f32[2,1,4,16,512]{4,3,2,1,0:T(8,128)S(1)}, f32[2,1,4,16,512]{4,3,2,1,0:T(8,128)}, u32[]{:S(2)}) copy-start(f32[2,1,4,16,512]{4,3,2,1,0:T(8,128)} %first.1) | copy-start | bytes 786436
  83.3 2.0 %copy-start.1 = (f32[2,1,4,16,512]{4,3,2,1,0:T(8,128)S(1)}, f32[2,1,4,16,512]{4,3,2,1,0:T(8,128)}, u32[]{:S(2)}) copy-start(f32[2,1,4,16,512]{4,3,2,1,0:T(8,128)} %second.1) | copy-start | bytes 786436
  83.3 2.0 %copy-start.2 = (bf16[2,4,16,512]{3,2,1,0:T(8,128)(2,1)S(1)}, bf16[2,4,16,512]{3,2,1,0:T(8,128)(2,1)}, u32[]{:S(2)}) copy-start(bf16[2,4,16,512]{3,2,1,0:T(8,128)(2,1)} %get-tuple-element.6) | copy-start | bytes 393220

commit v5 on v4

--- a/solution.py
+++ b/solution.py
@@ -81,7 +81,9 @@
         Q[:, lo:hi] = q.astype(BF16)
         if k < blocks - 1:
             U = mm(inverse, A[lo:hi, hi:], 1, 0)
-            A[hi:, hi:] = A[hi:, hi:] - mm(U, U, 0, 0)
+            for at in range(hi, A.shape[0], BLK):
+                u = U[:, at - hi :]
+                A[at : at + BLK, at:] = A[at : at + BLK, at:] - mm(u[:, 0:BLK], u, 0, 0)
             X[:, hi:] = X[:, hi:] - mm3(q, U, 1, 0)
 
 
@@ -130,18 +132,20 @@
     def y_send(i):
         what = [
             (fblock(xh, y), up), (fblock(xh, y), down), (fblock(xh, y), mirror),
-            (fblock(1 - xh, y), up), (fblock(1 - xh, y), down),
+            (fblock(1 - xh, y, 64, 64), up), (fblock(1 - xh, y, 64, 64), down),
             (fblock(xh, y - 1, 0, 64), up), (fblock(xh, y + 1, 64, 64), down),
             (fblock(1 - xh, y - 1, 0, 64), up), (fblock(1 - xh, y + 1, 64, 64), down),
+            (fblock(xh, y - 1, 0, 64), mirror), (fblock(xh, y + 1, 0, 64), mirror),
         ][i]
         return remote(what[0], what[0], ys.at[i], yr.at[i], what[1])
 
     def y_recv(i):
         what = [
             fblock(xh, y - 1), fblock(xh, y + 1), fblock(1 - xh, y),
-            fblock(1 - xh, y - 1), fblock(1 - xh, y + 1),
+            fblock(1 - xh, y - 1, 64, 64), fblock(1 - xh, y + 1, 64, 64),
             fblock(xh, y - 2, 0, 64), fblock(xh, y + 2, 64, 64),
             fblock(1 - xh, y - 2, 0, 64), fblock(1 - xh, y + 2, 64, 64),
+            fblock(1 - xh, y - 1, 0, 64), fblock(1 - xh, y + 1, 0, 64),
         ][i]
         remote(what, what, ys.at[i], yr.at[i], up).wait_recv()
 
@@ -285,31 +289,31 @@
         remote(MT.at[i], place(h, k), tws.at[1 + i], twr.at[1 + i], to).wait_recv()
     m_start()
 
-    y_recv(2)
-    y_send(3).start()
-    y_send(4).start()
-
-    def gram(h, yy):
-        part = fblock(h, yy)[...]
-        return mm(part, part, 0, 0)
-
-    A[...] = gram(xh, y) + gram(1 - xh, y)
-    r_start()
-    y_recv(0)
-    y_send(5).start()
-    y_recv(1)
-    y_send(6).start()
-    A[...] = A[...] + (gram(xh, y - 1) + gram(xh, y + 1))
-    y_recv(3)
-    y_send(7).start()
+    def gram(yy, add):
+        part = jnp.concatenate([fblock(xh, yy)[...], fblock(1 - xh, yy)[...]], axis=0)
+        for lo in range(0, part.shape[1], BLK):
+            product = mm(part[:, lo : lo + BLK], part[:, lo:], 0, 0)
+            A[lo : lo + BLK, lo:] = A[lo : lo + BLK, lo:] + product if add else product
+
+    for arrived, sends in ((2, (3, 4)), (0, (5, 9)), (1, (6, 10))):
+        y_recv(arrived)
+        for i in sends:
+            y_send(i).start()
+    gram(y, False)
     y_recv(4)
     y_send(8).start()
-    A[...] = A[...] + (gram(1 - xh, y - 1) + gram(1 - xh, y + 1))
+    y_recv(9)
+    y_send(7).start()
+    r_start()
+    y_recv(3)
+    gram(y - 1, True)
+    y_recv(10)
+    gram(y + 1, True)
     m_step(1)
     for i in range(5, 9):
         y_recv(i)
-    A[...] = A[...] + (gram(xh, y + 2) + gram(1 - xh, y + 2))
-    for i in range(9):
+    gram(y + 2, True)
+    for i in range(11):
         y_send(i).wait_send()
 
     hooks = {
@@ -454,7 +458,7 @@
             pltpu.VMEM((4, capacity, ROWS, rank // 2), BF16),
             pltpu.VMEM((3, capacity, 2, ROWS, rank // 2), BF16),
             dma((5,)), dma((8,)), dma((8,)), dma((8,)), dma((8,)),
-            dma((9,)), dma((9,)), dma((4,)), dma((4,)), dma((7,)), dma((7,)),
+            dma((11,)), dma((11,)), dma((4,)), dma((4,)), dma((7,)), dma((7,)),
             dma((7,)), dma((7,)), dma((9,)), dma((9,)), dma((7,)), dma((7,)), dma((3,)), dma((3,)),
         ],
         compiler_params=pltpu.CompilerParams(

time: 86.4 us -> 85.2 us (0.986)
  Pallas kernels: 80.2 us -> 78.9 us
    pallas_call x1, Pallas kernels: 80.2 us -> 78.9 us  [shards(): pl.pallas_call(kernel, out_shape=(pltpu.VMEM((matrices, local_rows, featu...]
where the time goes in v5:
time: 85.2 us; the launch traced here: 85 us
  Pallas kernels  78.9 us (93%)
  other arithmetic  3.3 us (4%)
  local copies, waits for them, and re-layouts  2.11 us (2%)
    pallas_call x1, Pallas kernels, shards(): pl.pallas_call(kernel, out_shape=(pltpu.VMEM((matrices, local_rows, featu...  78.9 us
    unnamed x9, local copies, waits for them, and re-layouts  2.04 us

profile of v5, /device:TPU:1, one launch (start us, length us, event | category | flops | bytes accessed | tf_op | source)
XLA Modules:
  0.0 85.0 jit_solution(17285440351106006943)
XLA Ops:
  0.7 0.9 %convert_reduce_fusion = s32[2,64]{1,0:T(2,128)S(1)} fusion(s32[2,64]{1,0:T(2,128)} %param.7, pred[64,64]{1,0:T(8,128)(4,1)S(1)} %iota_compare_fusion.1), kind=kLoop, calls=%fused_computation.13 | loop fusion | flops 32640 | bytes 5120 | tf_op jit(solution)/shard_map/reduce_sum | solution.py:420
  1.6 0.7 multiply_add_fusion.slots
  2.3 0.0 copy-start.3
  2.3 0.1 fusion.6
  2.4 0.1 constant_dynamic-slice_fusion
  2.5 0.7 select_reduce_fusion.bucket_of
  3.1 0.0 copy-done.3
  3.1 78.9 %shard_map.76 = (bf16[2,1024,1024]{2,1,0:T(8,128)(2,1)S(1)}, bf16[2,4,16,512]{3,2,1,0:T(8,128)(2,1)}) custom-call(s32[2,64]{1,0:T(2,128)} %copy-done.3, s32[2,128]{1,0:T(2,128)} %select_reduce_fusion.bucket_of, bf16[1,2,1024,1024]{3,2,1,0:T(8,128)(2,1)} %grads.1, f32[2,128,512]{2,1,0:T(8,128)} %raw.1, f32[2,1,4,16,512]{4,3,2,1,0:T(8,128)} %first.1, ...), custom_call_target="tpu_custom_call" | custom-call | flops 10000000000 | bytes 16000000 | tf_op jit(solution)/shard_map/pallas_call | solution.py:431
  82.0 0.0 copy-start
  82.0 0.0 copy-start.1
  82.0 0.0 copy-start.2
  82.1 2.0 %copy.13 = bf16[2,1024,1024]{2,1,0:T(8,128)(2,1)} copy(bf16[2,1024,1024]{2,1,0:T(8,128)(2,1)S(1)} %get-tuple-element.15) | data formatting | bytes 8388608
  84.1 0.0 copy-done
  84.1 0.0 copy-done.1
  84.1 0.0 copy-done.2
  84.1 0.9 %fusion.5 = (f32[2,1,4,16,512]{4,3,2,1,0:T(8,128)}, f32[2,1,4,16,512]{4,3,2,1,0:T(8,128)}) fusion(bf16[2,4,16,512]{3,2,1,0:T(8,128)(2,1)S(1)} %copy-done.2, f32[2,1,4,16,512]{4,3,2,1,0:T(8,128)S(1)} %copy-done.1, pred[2,4]{1,0:T(4,128)(4,1)S(1)} %constant_dynamic-slice_fusion, f32[2,1,4,16,512]{4,3,2,1,0:T(8,128)S(1)} %copy-done), kind=kLoop, calls=%fused_computation.7 | loop fusion | flops 655360 | bytes 1179656
  (1 shorter events, 0.0 us)
Async XLA Ops:
  2.3 0.8 copy-start.3
  82.0 2.1 %copy-start = (f32[2,1,4,16,512]{4,3,2,1,0:T(8,128)S(1)}, f32[2,1,4,16,512]{4,3,2,1,0:T(8,128)}, u32[]{:S(2)}) copy-start(f32[2,1,4,16,512]{4,3,2,1,0:T(8,128)} %first.1) | copy-start | bytes 786436
  82.0 2.0 %copy-start.1 = (f32[2,1,4,16,512]{4,3,2,1,0:T(8,128)S(1)}, f32[2,1,4,16,512]{4,3,2,1,0:T(8,128)}, u32[]{:S(2)}) copy-start(f32[2,1,4,16,512]{4,3,2,1,0:T(8,128)} %second.1) | copy-start | bytes 786436
  82.0 2.0 %copy-start.2 = (bf16[2,4,16,512]{3,2,1,0:T(8,128)(2,1)S(1)}, bf16[2,4,16,512]{3,2,1,0:T(8,128)(2,1)}, u32[]{:S(2)}) copy-start(bf16[2,4,16,512]{3,2,1,0:T(8,128)(2,1)} %get-tuple-element.6) | copy-start | bytes 393220

commit v6 on v5

--- a/solution.py
+++ b/solution.py
@@ -279,15 +279,15 @@
     for i in range(3):
         y_send(i).start()
     t_grads = remote(grads.at[0, 1 - c], T, tws.at[0], twr.at[0], twin)
-    t_grads.start()
     for i in range(3):
         moments_to(i).start()
+    t_grads.start()
+    for i, (to, h, k) in enumerate(targets):
+        remote(MT.at[i], place(h, k), tws.at[1 + i], twr.at[1 + i], to).wait_recv()
+    m_start()
     own_grads.wait()
     t_grads.wait_recv()
     x_start()
-    for i, (to, h, k) in enumerate(targets):
-        remote(MT.at[i], place(h, k), tws.at[1 + i], twr.at[1 + i], to).wait_recv()
-    m_start()
 
     def gram(yy, add):
         part = jnp.concatenate([fblock(xh, yy)[...], fblock(1 - xh, yy)[...]], axis=0)
@@ -304,12 +304,12 @@
     y_send(8).start()
     y_recv(9)
     y_send(7).start()
+    m_step(1)
     r_start()
     y_recv(3)
     gram(y - 1, True)
     y_recv(10)
     gram(y + 1, True)
-    m_step(1)
     for i in range(5, 9):
         y_recv(i)
     gram(y + 2, True)
@@ -317,13 +317,14 @@
         y_send(i).wait_send()
 
     hooks = {
-        0: {0: lambda: r_step(1), 4: lambda: m_step(2), 7: lambda: r_step(2)},
-        1: {3: lambda: m_step(3), 6: lambda: r_step(3)},
-        2: {3: r_last, 6: lambda: m_step(4)},
-        3: {4: r_sum},
+        0: {2: lambda: r_step(1), 6: lambda: m_step(2)},
+        1: {2: lambda: r_step(2)},
+        2: {0: lambda: r_step(3), 3: lambda: m_step(3), 7: r_last},
+        3: {7: r_sum},
     }
     factor(A, X, S, Q, hooks)
     g_start()
+    m_step(4)
 
     for lo in range(0, Q.shape[1], BLK):
         QT[lo : lo + BLK, :] = Q[:, lo : lo + BLK].T

time: 85.2 us -> 82.7 us (0.971)
  Pallas kernels: 78.9 us -> 76.4 us
    pallas_call x1, Pallas kernels: 78.9 us -> 76.4 us  [shards(): pl.pallas_call(kernel, out_shape=(pltpu.VMEM((matrices, local_rows, featu...]
where the time goes in v6:
time: 82.7 us; the launch traced here: 82.5 us
  Pallas kernels  76.4 us (92%)
  other arithmetic  3.3 us (4%)
  local copies, waits for them, and re-layouts  2.11 us (3%)
    pallas_call x1, Pallas kernels, shards(): pl.pallas_call(kernel, out_shape=(pltpu.VMEM((matrices, local_rows, featu...  76.4 us
    unnamed x9, local copies, waits for them, and re-layouts  2.04 us

profile of v6, /device:TPU:1, one launch (start us, length us, event | category | flops | bytes accessed | tf_op | source)
XLA Modules:
  0.0 82.5 jit_solution(4466450053975695271)
XLA Ops:
  0.7 0.9 %convert_reduce_fusion = s32[2,64]{1,0:T(2,128)S(1)} fusion(s32[2,64]{1,0:T(2,128)} %param.7, pred[64,64]{1,0:T(8,128)(4,1)S(1)} %iota_compare_fusion.1), kind=kLoop, calls=%fused_computation.13 | loop fusion | flops 32640 | bytes 5120 | tf_op jit(solution)/shard_map/reduce_sum | solution.py:421
  1.6 0.7 multiply_add_fusion.slots
  2.3 0.0 copy-start.3
  2.3 0.1 fusion.6
  2.4 0.1 constant_dynamic-slice_fusion
  2.5 0.7 select_reduce_fusion.bucket_of
  3.1 0.0 copy-done.3
  3.1 76.4 %shard_map.76 = (bf16[2,1024,1024]{2,1,0:T(8,128)(2,1)S(1)}, bf16[2,4,16,512]{3,2,1,0:T(8,128)(2,1)}) custom-call(s32[2,64]{1,0:T(2,128)} %copy-done.3, s32[2,128]{1,0:T(2,128)} %select_reduce_fusion.bucket_of, bf16[1,2,1024,1024]{3,2,1,0:T(8,128)(2,1)} %grads.1, f32[2,128,512]{2,1,0:T(8,128)} %raw.1, f32[2,1,4,16,512]{4,3,2,1,0:T(8,128)} %first.1, ...), custom_call_target="tpu_custom_call" | custom-call | flops 10000000000 | bytes 16000000 | tf_op jit(solution)/shard_map/pallas_call | solution.py:432
  79.5 0.0 copy-start
  79.5 0.0 copy-start.1
  79.5 0.0 copy-start.2
  79.5 2.0 %copy.13 = bf16[2,1024,1024]{2,1,0:T(8,128)(2,1)} copy(bf16[2,1024,1024]{2,1,0:T(8,128)(2,1)S(1)} %get-tuple-element.15) | data formatting | bytes 8388608
  81.6 0.0 copy-done
  81.6 0.0 copy-done.1
  81.6 0.0 copy-done.2
  81.6 0.9 %fusion.5 = (f32[2,1,4,16,512]{4,3,2,1,0:T(8,128)}, f32[2,1,4,16,512]{4,3,2,1,0:T(8,128)}) fusion(bf16[2,4,16,512]{3,2,1,0:T(8,128)(2,1)S(1)} %copy-done.2, f32[2,1,4,16,512]{4,3,2,1,0:T(8,128)S(1)} %copy-done.1, pred[2,4]{1,0:T(4,128)(4,1)S(1)} %constant_dynamic-slice_fusion, f32[2,1,4,16,512]{4,3,2,1,0:T(8,128)S(1)} %copy-done), kind=kLoop, calls=%fused_computation.7 | loop fusion | flops 655360 | bytes 1179656
  (1 shorter events, 0.0 us)
Async XLA Ops:
  2.3 0.8 %copy-start.3 = (s32[2,64]{1,0:T(2,128)}, s32[2,64]{1,0:T(2,128)S(1)}, u32[]{:S(2)}) copy-start(s32[2,64]{1,0:T(2,128)S(1)} %multiply_add_fusion.slots) | copy-start | bytes 1540
  79.5 2.1 %copy-start = (f32[2,1,4,16,512]{4,3,2,1,0:T(8,128)S(1)}, f32[2,1,4,16,512]{4,3,2,1,0:T(8,128)}, u32[]{:S(2)}) copy-start(f32[2,1,4,16,512]{4,3,2,1,0:T(8,128)} %first.1) | copy-start | bytes 786436
  79.5 2.0 %copy-start.1 = (f32[2,1,4,16,512]{4,3,2,1,0:T(8,128)S(1)}, f32[2,1,4,16,512]{4,3,2,1,0:T(8,128)}, u32[]{:S(2)}) copy-start(f32[2,1,4,16,512]{4,3,2,1,0:T(8,128)} %second.1) | copy-start | bytes 786436
  79.5 2.0 %copy-start.2 = (bf16[2,4,16,512]{3,2,1,0:T(8,128)(2,1)S(1)}, bf16[2,4,16,512]{3,2,1,0:T(8,128)(2,1)}, u32[]{:S(2)}) copy-start(bf16[2,4,16,512]{3,2,1,0:T(8,128)(2,1)} %get-tuple-element.6) | copy-start | bytes 393220

commit v7 on v6

--- a/solution.py
+++ b/solution.py
@@ -317,12 +317,13 @@
         y_send(i).wait_send()
 
     hooks = {
-        0: {2: lambda: r_step(1), 6: lambda: m_step(2)},
-        1: {2: lambda: r_step(2)},
-        2: {0: lambda: r_step(3), 3: lambda: m_step(3), 7: r_last},
-        3: {7: r_sum},
+        0: {3: lambda: r_step(1), 7: lambda: m_step(2)},
+        1: {4: lambda: r_step(2)},
+        2: {2: lambda: r_step(3), 5: lambda: m_step(3)},
+        3: {1: r_last},
     }
     factor(A, X, S, Q, hooks)
+    r_sum()
     g_start()
     m_step(4)
 
@@ -417,9 +418,12 @@
     capacity = first_moment.shape[2]
     slot_total = lax.axis_size("dp") * capacity
     same = bucket_owner[:, :, None] == bucket_owner[:, None, :]
-    earlier = jnp.arange(buckets)[None, :] < jnp.arange(buckets)[:, None]
-    ranks = jnp.sum(jnp.logical_and(same, earlier).astype(jnp.int32), axis=-1)
-    slots = bucket_owner * capacity + ranks
+    index = jnp.arange(buckets)
+    earlier = index[None, :] < index[:, None]
+    terms = jnp.logical_and(same, earlier).astype(jnp.int32) + jnp.where(
+        index[None, :] == index[:, None], capacity * bucket_owner[:, None, :], 0
+    )
+    slots = jnp.sum(terms, axis=-1)
     matches = slots[:, None, :] == jnp.arange(slot_total, dtype=jnp.int32)[None, :, None]
     occupied = jnp.any(matches, axis=2)
     bucket_of = jnp.sum(

time: 82.7 us -> 81.9 us (level)
  no operation moved by 1% of the time
where the time goes in v7:
time: 81.9 us; the launch traced here: 81.7 us
  Pallas kernels  75.6 us (92%)
  other arithmetic  3.31 us (4%)
  local copies, waits for them, and re-layouts  2.12 us (3%)
    pallas_call x1, Pallas kernels, shards(): pl.pallas_call(kernel, out_shape=(pltpu.VMEM((matrices, local_rows, featu...  75.6 us
    unnamed x9, local copies, waits for them, and re-layouts  2.04 us

profile of v7, /device:TPU:1, one launch (start us, length us, event | category | flops | bytes accessed | tf_op | source)
XLA Modules:
  0.0 81.7 jit_solution(13595231641944652128)
XLA Ops:
  0.6 0.7 broadcast_multiply_fusion
  1.3 0.9 %add_reduce_fusion.slots = s32[2,64]{1,0:T(2,128)S(1)} fusion(s32[2,64]{1,0:T(2,128)S(1)} %broadcast_multiply_fusion, s32[2,64]{1,0:T(2,128)} %param.7, pred[64,64]{1,0:T(8,128)(4,1)S(1)} %get-tuple-element.15, pred[64,64]{1,0:T(8,128)(4,1)S(1)} %get-tuple-element.16), kind=kLoop, calls=%fused_computation.13 | loop fusion | flops 49024 | bytes 9728 | tf_op jit(solution)/shard_map/reduce_sum | solution.py:426
  2.3 0.0 copy-start.3
  2.3 0.1 fusion.6
  2.4 0.1 constant_dynamic-slice_fusion
  2.5 0.7 select_reduce_fusion.bucket_of
  3.1 0.0 copy-done.3
  3.1 75.6 %shard_map.76 = (bf16[2,1024,1024]{2,1,0:T(8,128)(2,1)S(1)}, bf16[2,4,16,512]{3,2,1,0:T(8,128)(2,1)}) custom-call(s32[2,64]{1,0:T(2,128)} %copy-done.3, s32[2,128]{1,0:T(2,128)} %select_reduce_fusion.bucket_of, bf16[1,2,1024,1024]{3,2,1,0:T(8,128)(2,1)} %grads.1, f32[2,128,512]{2,1,0:T(8,128)} %raw.1, f32[2,1,4,16,512]{4,3,2,1,0:T(8,128)} %first.1, ...), custom_call_target="tpu_custom_call" | custom-call | flops 10000000000 | bytes 16000000 | tf_op jit(solution)/shard_map/pallas_call | solution.py:436
  78.7 0.0 copy-start
  78.7 0.0 copy-start.1
  78.7 0.0 copy-start.2
  78.8 2.0 %copy.13 = bf16[2,1024,1024]{2,1,0:T(8,128)(2,1)} copy(bf16[2,1024,1024]{2,1,0:T(8,128)(2,1)S(1)} %get-tuple-element.17) | data formatting | bytes 8388608
  80.8 0.0 copy-done
  80.8 0.0 copy-done.1
  80.8 0.0 copy-done.2
  80.8 0.9 %fusion.5 = (f32[2,1,4,16,512]{4,3,2,1,0:T(8,128)}, f32[2,1,4,16,512]{4,3,2,1,0:T(8,128)}) fusion(bf16[2,4,16,512]{3,2,1,0:T(8,128)(2,1)S(1)} %copy-done.2, f32[2,1,4,16,512]{4,3,2,1,0:T(8,128)S(1)} %copy-done.1, pred[2,4]{1,0:T(4,128)(4,1)S(1)} %constant_dynamic-slice_fusion, f32[2,1,4,16,512]{4,3,2,1,0:T(8,128)S(1)} %copy-done), kind=kLoop, calls=%fused_computation.7 | loop fusion | flops 655360 | bytes 1179656
  (1 shorter events, 0.0 us)
Async XLA Ops:
  2.3 0.9 %copy-start.3 = (s32[2,64]{1,0:T(2,128)}, s32[2,64]{1,0:T(2,128)S(1)}, u32[]{:S(2)}) copy-start(s32[2,64]{1,0:T(2,128)S(1)} %add_reduce_fusion.slots) | copy-start | bytes 1540
  78.7 2.1 %copy-start = (f32[2,1,4,16,512]{4,3,2,1,0:T(8,128)S(1)}, f32[2,1,4,16,512]{4,3,2,1,0:T(8,128)}, u32[]{:S(2)}) copy-start(f32[2,1,4,16,512]{4,3,2,1,0:T(8,128)} %first.1) | copy-start | bytes 786436
  78.7 2.0 %copy-start.1 = (f32[2,1,4,16,512]{4,3,2,1,0:T(8,128)S(1)}, f32[2,1,4,16,512]{4,3,2,1,0:T(8,128)}, u32[]{:S(2)}) copy-start(f32[2,1,4,16,512]{4,3,2,1,0:T(8,128)} %second.1) | copy-start | bytes 786436
  78.7 2.0 %copy-start.2 = (bf16[2,4,16,512]{3,2,1,0:T(8,128)(2,1)S(1)}, bf16[2,4,16,512]{3,2,1,0:T(8,128)(2,1)}, u32[]{:S(2)}) copy-start(bf16[2,4,16,512]{3,2,1,0:T(8,128)(2,1)} %get-tuple-element.6) | copy-start | bytes 393220

commit v8 on v7

--- a/solution.py
+++ b/solution.py
@@ -28,7 +28,8 @@
 def mm3(a, b, ca, cb):
     ah, bh = a.astype(BF16), b.astype(BF16)
     al, bl = (a - ah.astype(F32)).astype(BF16), (b - bh.astype(F32)).astype(BF16)
-    return mm(ah, bh, ca, cb, None) + (mm(ah, bl, ca, cb, None) + mm(al, bh, ca, cb, None))
+    left = jnp.concatenate([ah, ah, al], axis=ca)
+    return mm(left, jnp.concatenate([bh, bl, bh], axis=cb), ca, cb, None)
 
 
 def panel(S, g):

time: 81.9 us -> 81.6 us (level)
  no operation moved by 1% of the time
where the time goes in v8:
time: 81.6 us; the launch traced here: 81.4 us
  Pallas kernels  75.3 us (92%)
  other arithmetic  3.31 us (4%)
  local copies, waits for them, and re-layouts  2.12 us (3%)
    pallas_call x1, Pallas kernels, shards(): pl.pallas_call(kernel, out_shape=(pltpu.VMEM((matrices, local_rows, featu...  75.3 us
    unnamed x9, local copies, waits for them, and re-layouts  2.04 us

profile of v8, /device:TPU:1, one launch (start us, length us, event | category | flops | bytes accessed | tf_op | source)
XLA Modules:
  0.0 81.4 jit_solution(1818078645694482093)
XLA Ops:
  0.6 0.7 broadcast_multiply_fusion
  1.3 0.9 %add_reduce_fusion.slots = s32[2,64]{1,0:T(2,128)S(1)} fusion(s32[2,64]{1,0:T(2,128)S(1)} %broadcast_multiply_fusion, s32[2,64]{1,0:T(2,128)} %param.7, pred[64,64]{1,0:T(8,128)(4,1)S(1)} %get-tuple-element.15, pred[64,64]{1,0:T(8,128)(4,1)S(1)} %get-tuple-element.16), kind=kLoop, calls=%fused_computation.13 | loop fusion | flops 49024 | bytes 9728 | tf_op jit(solution)/shard_map/reduce_sum | solution.py:427
  2.3 0.0 copy-start.3
  2.3 0.1 fusion.6
  2.4 0.1 constant_dynamic-slice_fusion
  2.5 0.7 select_reduce_fusion.bucket_of
  3.1 0.0 copy-done.3
  3.1 75.3 %shard_map.76 = (bf16[2,1024,1024]{2,1,0:T(8,128)(2,1)S(1)}, bf16[2,4,16,512]{3,2,1,0:T(8,128)(2,1)}) custom-call(s32[2,64]{1,0:T(2,128)} %copy-done.3, s32[2,128]{1,0:T(2,128)} %select_reduce_fusion.bucket_of, bf16[1,2,1024,1024]{3,2,1,0:T(8,128)(2,1)} %grads.1, f32[2,128,512]{2,1,0:T(8,128)} %raw.1, f32[2,1,4,16,512]{4,3,2,1,0:T(8,128)} %first.1, ...), custom_call_target="tpu_custom_call" | custom-call | flops 10000000000 | bytes 16000000 | tf_op jit(solution)/shard_map/pallas_call | solution.py:437
  78.5 0.0 copy-start
  78.5 0.0 copy-start.1
  78.5 0.0 copy-start.2
  78.5 2.0 %copy.13 = bf16[2,1024,1024]{2,1,0:T(8,128)(2,1)} copy(bf16[2,1024,1024]{2,1,0:T(8,128)(2,1)S(1)} %get-tuple-element.17) | data formatting | bytes 8388608
  80.5 0.0 copy-done
  80.5 0.0 copy-done.1
  80.5 0.0 copy-done.2
  80.5 0.9 %fusion.5 = (f32[2,1,4,16,512]{4,3,2,1,0:T(8,128)}, f32[2,1,4,16,512]{4,3,2,1,0:T(8,128)}) fusion(bf16[2,4,16,512]{3,2,1,0:T(8,128)(2,1)S(1)} %copy-done.2, f32[2,1,4,16,512]{4,3,2,1,0:T(8,128)S(1)} %copy-done.1, pred[2,4]{1,0:T(4,128)(4,1)S(1)} %constant_dynamic-slice_fusion, f32[2,1,4,16,512]{4,3,2,1,0:T(8,128)S(1)} %copy-done), kind=kLoop, calls=%fused_computation.7 | loop fusion | flops 655360 | bytes 1179656
  (1 shorter events, 0.0 us)
Async XLA Ops:
  2.3 0.9 %copy-start.3 = (s32[2,64]{1,0:T(2,128)}, s32[2,64]{1,0:T(2,128)S(1)}, u32[]{:S(2)}) copy-start(s32[2,64]{1,0:T(2,128)S(1)} %add_reduce_fusion.slots) | copy-start | bytes 1540
  78.5 2.1 %copy-start = (f32[2,1,4,16,512]{4,3,2,1,0:T(8,128)S(1)}, f32[2,1,4,16,512]{4,3,2,1,0:T(8,128)}, u32[]{:S(2)}) copy-start(f32[2,1,4,16,512]{4,3,2,1,0:T(8,128)} %first.1) | copy-start | bytes 786436
  78.5 2.0 %copy-start.1 = (f32[2,1,4,16,512]{4,3,2,1,0:T(8,128)S(1)}, f32[2,1,4,16,512]{4,3,2,1,0:T(8,128)}, u32[]{:S(2)}) copy-start(f32[2,1,4,16,512]{4,3,2,1,0:T(8,128)} %second.1) | copy-start | bytes 786436
  78.5 2.0 %copy-start.2 = (bf16[2,4,16,512]{3,2,1,0:T(8,128)(2,1)S(1)}, bf16[2,4,16,512]{3,2,1,0:T(8,128)(2,1)}, u32[]{:S(2)}) copy-start(bf16[2,4,16,512]{3,2,1,0:T(8,128)(2,1)} %get-tuple-element.6) | copy-start | bytes 393220
